TPU v7x, 32 devices: a whole 2x2x4 slice. The times are simulated.
32 devices in a mesh: req: 8 (over z, x), tp: 4 (over y, core).
Axes of the slice: x: 2, y: 2, z: 4, core: 2. Of those that a mesh axis runs over, the one named last changes fastest.
Arguments:
- tokens: bfloat16 [2048, 1280], P('req'), as said below
- attention_gain: bfloat16 [1280], replicated, may hold values from 0.099609375 to 1.8984375
- feedforward_gain: bfloat16 [1280], replicated, may hold values from 0.099609375 to 1.8984375
- query_weight: bfloat16 [1280, 1280], P(None, 'tp'), may hold values from -0.15625 to 0.15625
- key_weight: bfloat16 [1280, 1280], P(None, 'tp'), may hold values from -0.625 to 0.625
- value_weight: bfloat16 [1280, 1280], P(None, 'tp'), may hold values from -0.3125 to 0.3125
- out_weight: bfloat16 [1280, 1280], P('tp'), may hold values from -0.3125 to 0.3125
- up_weight: bfloat16 [1280, 1280], P(None, 'tp'), may hold values from -0.15625 to 0.15625
- down_weight: bfloat16 [1280, 1280], P('tp'), may hold values from -0.15625 to 0.15625
- cache_keys: bfloat16 [8, 16, 192, 1280], P('req', None, None, 'tp'), as said below
- cache_values: bfloat16 [8, 16, 192, 1280], P('req', None, None, 'tp'), may hold values from -12 to 12
- request_prefix: int32 [16], replicated, may hold values from 0 to 15
- suffix_length: int32 [16], replicated, may hold values from 1 to 128, as said below
Outputs:
- layer_out: bfloat16 [2048, 1280], P('req', 'tp')
Inputs may be any that keep to these rules, and one draw needn't show every extreme that they name: `suffix_length`: requests d * 2 to d * 2 + 1 are those of index d of req; their lengths sum to at most 192, on some index exactly 192; some request has exactly 128. `cache_keys`: keys of the cached prefix patches. `tokens`: patch embeddings.
All inputs are finite; a program needn't handle non-finite values.
Results may differ from a plain program's by a relative error of at most 0.0055.
The roundings to bfloat16 on the way count: a program that leaves them out, or rounds other values in their place, can miss the bound.
Values may be sent and summed in bfloat16 or wider, within the bound.
A program may use at most 128 MiB of HBM per device.

v0:
```python
import math

import jax
import jax.numpy as jnp
from jax import lax
from jax.sharding import PartitionSpec as P

HDIM = 80
SLOT = 128
R_DEV = 2
PG = 192


EPSILON = 1e-06
NEGATIVE = -1e30


def normalize(values, gain):
    floats = values.astype(jnp.float32)
    mean_square = jnp.mean(floats * floats, axis=-1, keepdims=True)
    return (floats * lax.rsqrt(mean_square + EPSILON) * gain.astype(jnp.float32)).astype(
        jnp.bfloat16
    )


def owner_partial(query_block, key_block, value_block, score_scale):
    scores = (
        jnp.einsum("bqhe,bkhe->bhqk", query_block, key_block, preferred_element_type=jnp.float32)
        * score_scale
    )
    top_value = lax.optimization_barrier(jnp.max(scores, axis=-1).astype(jnp.bfloat16))
    weights = jnp.exp(scores - top_value.astype(jnp.float32)[..., None])
    total_mass = jnp.sum(weights, axis=-1)
    numerator = jnp.einsum(
        "bhqk,bkhe->bqhe",
        weights.astype(jnp.bfloat16),
        value_block,
        preferred_element_type=jnp.float32,
    )
    total_rows = jnp.transpose(total_mass, (0, 2, 1))
    share_rows = (numerator / total_rows[..., None]).astype(jnp.bfloat16)
    return (share_rows, jnp.transpose(top_value, (0, 2, 1)), total_rows.astype(jnp.bfloat16))


def block_count(item_count, row_count):
    group_size = 1
    while group_size * row_count < 512 and item_count % (group_size * 2) == 0:
        group_size = group_size * 2
    return group_size


def per_device(
    tokens,
    attention_gain,
    feedforward_gain,
    query_weight,
    key_weight,
    value_weight,
    out_weight,
    up_weight,
    down_weight,
    cache_keys,
    cache_values,
    request_prefix,
    suffix_length,
):
    owners = lax.axis_size("req")
    local_rows = tokens.shape[0]
    local_width = query_weight.shape[1]
    heads_local = local_width // HDIM
    score_scale = 1.0 / math.sqrt(HDIM)
    normed = normalize(tokens, attention_gain)
    queries = jnp.dot(normed, query_weight, preferred_element_type=jnp.float32).astype(jnp.bfloat16)
    keys_own = jnp.dot(normed, key_weight, preferred_element_type=jnp.float32).astype(jnp.bfloat16)
    values_own = jnp.dot(normed, value_weight, preferred_element_type=jnp.float32).astype(
        jnp.bfloat16
    )
    own_lengths = lax.dynamic_slice_in_dim(suffix_length, lax.axis_index("req") * R_DEV, R_DEV)
    query_slots = queries.reshape(R_DEV, SLOT, heads_local, HDIM)
    key_slots = keys_own.reshape(R_DEV, SLOT, heads_local, HDIM)
    value_slots = values_own.reshape(R_DEV, SLOT, heads_local, HDIM)
    own_scores = (
        jnp.einsum("rqhe,rkhe->rhqk", query_slots, key_slots, preferred_element_type=jnp.float32)
        * score_scale
    )
    causal = jnp.arange(SLOT)[:, None] >= jnp.arange(SLOT)[None, :]
    own_scores = jnp.where(causal[None, None], own_scores, NEGATIVE)
    own_top = jnp.max(own_scores, axis=-1)
    own_weights = jnp.exp(own_scores - own_top[..., None])
    own_total = jnp.sum(own_weights, axis=-1)
    own_numer = jnp.einsum(
        "rhqk,rkhe->rqhe",
        own_weights.astype(jnp.bfloat16),
        value_slots,
        preferred_element_type=jnp.float32,
    )
    own_top = jnp.transpose(own_top, (0, 2, 1)).reshape(local_rows, heads_local)
    own_total = jnp.transpose(own_total, (0, 2, 1)).reshape(local_rows, heads_local)
    own_numer = own_numer.reshape(local_rows, heads_local, HDIM)
    prefix_count = cache_keys.shape[1]
    prefix_keys = cache_keys[0].reshape(prefix_count, PG, heads_local, HDIM)
    prefix_values = cache_values[0].reshape(prefix_count, PG, heads_local, HDIM)
    gathered = lax.all_gather(queries, "req", axis=0, tiled=True)
    requests = owners * R_DEV
    gathered = gathered.reshape(requests, SLOT, heads_local, HDIM)
    group_size = block_count(requests, SLOT)

    def padded_block(block_index):
        query_block = lax.dynamic_slice_in_dim(gathered, block_index * group_size, group_size, 0)
        chosen = lax.dynamic_slice_in_dim(request_prefix, block_index * group_size, group_size, 0)
        return owner_partial(query_block, prefix_keys[chosen], prefix_values[chosen], score_scale)

    shares, maxima, totals = lax.map(padded_block, jnp.arange(requests // group_size))
    shares = shares.reshape(owners * local_rows, local_width)
    maxima = maxima.reshape(owners * local_rows, heads_local)
    totals = totals.reshape(owners * local_rows, heads_local)
    shares, maxima, totals = (
        lax.all_to_all(shares, "req", split_axis=0, concat_axis=0, tiled=True),
        lax.all_to_all(maxima, "req", split_axis=0, concat_axis=0, tiled=True),
        lax.all_to_all(totals, "req", split_axis=0, concat_axis=0, tiled=True),
    )
    shares = shares.reshape(owners, local_rows, heads_local, HDIM)
    maxima = maxima.reshape(owners, local_rows, heads_local)
    totals = totals.reshape(owners, local_rows, heads_local)
    maxima = maxima.astype(jnp.float32)
    totals = totals.astype(jnp.float32)
    row_peak = jnp.maximum(own_top, jnp.max(maxima, axis=0))
    own_factor = jnp.exp(own_top - row_peak)
    far_factor = totals * jnp.exp(maxima - row_peak[None])
    denominator = own_total * own_factor + jnp.sum(far_factor, axis=0)
    numerator = own_numer * own_factor[..., None] + jnp.einsum(
        "oth,othe->the", far_factor, shares.astype(jnp.float32)
    )
    attention = (
        (numerator / denominator[..., None]).astype(jnp.bfloat16).reshape(local_rows, local_width)
    )
    head_terms = jnp.dot(attention, out_weight, preferred_element_type=jnp.float32)
    tensor_index = lax.axis_index("tp")
    summed = lax.psum(head_terms, "tp")
    middle = (tokens.astype(jnp.float32) + summed).astype(jnp.bfloat16)
    normed_middle = normalize(middle, feedforward_gain)
    middle_share = lax.dynamic_slice_in_dim(middle, tensor_index * local_width, local_width, 1)
    hidden = jax.nn.silu(
        jnp.dot(normed_middle, up_weight, preferred_element_type=jnp.float32)
    ).astype(jnp.bfloat16)
    down_terms = jnp.dot(hidden, down_weight, preferred_element_type=jnp.float32)
    down_share = lax.psum_scatter(down_terms, "tp", scatter_dimension=1, tiled=True)
    live_mask = jnp.arange(local_rows) % SLOT < jnp.repeat(
        own_lengths, SLOT, total_repeat_length=local_rows
    )
    result = jnp.where(live_mask[:, None], middle_share.astype(jnp.float32) + down_share, 0.0)
    return result.astype(jnp.bfloat16)


def solution(mesh):
    in_specs = (
        P("req", None),
        P(),
        P(),
        P(None, "tp"),
        P(None, "tp"),
        P(None, "tp"),
        P("tp", None),
        P(None, "tp"),
        P("tp", None),
        P("req", None, None, "tp"),
        P("req", None, None, "tp"),
        P(),
        P(),
    )
    out_specs = P("req", "tp")
    return jax.shard_map(
        per_device, mesh=mesh, in_specs=in_specs, out_specs=out_specs, check_vma=False
    )
```

profile of v0, /device:TPU:0, one launch (start us, length us, event | category | flops | bytes accessed | tf_op | source)
XLA Modules:
  0.0 236.7 jit_solution(10408065247713335690)
XLA Ops:
  6.5 1.4 copy.63
  8.2 1.2 convolution_convert_fusion.1
  9.5 3.0 %copy.69 = bf16[1,16,192,320]{2,3,1,0:T(8,128)(2,1)S(1)} copy(bf16[1,16,192,320]{3,2,1,0:T(8,128)(2,1)} %param.27) | data formatting | bytes 3932160 | tf_op args[10]
  12.5 4.3 %copy.71 = bf16[16,192,4,80]{3,2,1,0:T(4,128)(2,1)} copy(bf16[16,192,4,80]{1,3,2,0:T(8,128)(2,1)S(1)} %bitcast.103) | data formatting | bytes 3932160 | tf_op jit(solution)/shard_map/while | solution.py:113
  16.8 3.0 %copy.70 = bf16[1,16,192,320]{2,3,1,0:T(8,128)(2,1)S(1)} copy(bf16[1,16,192,320]{3,2,1,0:T(8,128)(2,1)} %param.26) | data formatting | bytes 3932160 | tf_op args[9]
  19.8 4.2 %copy.73 = bf16[16,192,4,80]{3,2,1,0:T(4,128)(2,1)} copy(bf16[16,192,4,80]{1,3,2,0:T(8,128)(2,1)S(1)} %bitcast.104) | data formatting | bytes 3932160 | tf_op jit(solution)/shard_map/while | solution.py:113
  24.0 30.5 %all-gather.2.cloned.1.call-done = bf16[2048,320]{0,1:T(8,128)(2,1)} async-done(((bf16[256,320]{0,1:T(8,128)(2,1)}), bf16[2048,320]{0,1:T(8,128)(2,1)}) %all-gather.2.cloned.1.call-update) | async-done | bytes 1310736 | tf_op jit(solution)/shard_map/all_gather | solution.py:103
  54.6 2.7 %copy.99 = bf16[40,8,16,128]{3,2,1,0:T(8,128)(2,1)} copy(bf16[40,8,16,128]{3,1,2,0:T(8,128)(2,1)} %bitcast.106) | data formatting | bytes 2621440
  57.3 46.5 %while.15 = (s32[]{:T(128)}, bf16[4,4,128,4,80]{2,1,0,4,3:T(4,128)(2,1)}, bf16[4,4,128,4]{2,3,1,0:T(4,128)(2,1)S(1)}, bf16[4,4,128,4]{2,3,1,0:T(4,128)(2,1)}, s3...) while((s32[]{:T(128)}, ...), condition=%wide.region_5.6_spmd, body=%wide.region_2.5_spmd.sunk | while | flops 128517136 | bytes 9707807 | solution.py:113
  57.3 0.6 dynamic_slice.26
  58.5 1.3 constant_dynamic-slice_fusion.2
  59.9 3.1 %gather_fusion = bf16[4,192,4,80]{3,2,1,0:T(4,128)(2,1)S(1)} fusion(bf16[16,192,4,80]{3,2,1,0:T(4,128)(2,1)} %get-tuple-element.234, s32[1024]{0:T(1024)S(1)} %pad_clamp_fusion.2), kind=kCustom, calls=%fused_computation.1.clone.1 | custom fusion | bytes 983056 | tf_op jit(solution)/shard_map/while/body/eval_jaxpr/gather | solution.py:111
  63.4 3.1 %gather_fusion.1 = bf16[4,192,4,80]{3,2,1,0:T(4,128)(2,1)S(1)} fusion(bf16[16,192,4,80]{3,2,1,0:T(4,128)(2,1)} %get-tuple-element.232, s32[1024]{0:T(1024)S(1)} %pad_clamp_fusion.2), kind=kCustom, calls=%fused_computation.clone.1 | custom fusion | bytes 983056 | tf_op jit(solution)/shard_map/while/body/eval_jaxpr/gather | solution.py:111
  67.3 1.0 copy_dynamic-update-slice_fusion.2
  68.9 0.6 dynamic_slice.26
  70.1 1.3 constant_dynamic-slice_fusion.2
  71.5 3.1 %gather_fusion = bf16[4,192,4,80]{3,2,1,0:T(4,128)(2,1)S(1)} fusion(bf16[16,192,4,80]{3,2,1,0:T(4,128)(2,1)} %get-tuple-element.234, s32[1024]{0:T(1024)S(1)} %pad_clamp_fusion.2), kind=kCustom, calls=%fused_computation.1.clone.1 | custom fusion | bytes 983056 | tf_op jit(solution)/shard_map/while/body/eval_jaxpr/gather | solution.py:111
  75.0 3.1 %gather_fusion.1 = bf16[4,192,4,80]{3,2,1,0:T(4,128)(2,1)S(1)} fusion(bf16[16,192,4,80]{3,2,1,0:T(4,128)(2,1)} %get-tuple-element.232, s32[1024]{0:T(1024)S(1)} %pad_clamp_fusion.2), kind=kCustom, calls=%fused_computation.clone.1 | custom fusion | bytes 983056 | tf_op jit(solution)/shard_map/while/body/eval_jaxpr/gather | solution.py:111
  78.9 1.0 copy_dynamic-update-slice_fusion.2
  80.5 0.6 dynamic_slice.26
  81.7 1.3 constant_dynamic-slice_fusion.2
  83.1 3.1 %gather_fusion = bf16[4,192,4,80]{3,2,1,0:T(4,128)(2,1)S(1)} fusion(bf16[16,192,4,80]{3,2,1,0:T(4,128)(2,1)} %get-tuple-element.234, s32[1024]{0:T(1024)S(1)} %pad_clamp_fusion.2), kind=kCustom, calls=%fused_computation.1.clone.1 | custom fusion | bytes 983056 | tf_op jit(solution)/shard_map/while/body/eval_jaxpr/gather | solution.py:111
  86.6 3.1 %gather_fusion.1 = bf16[4,192,4,80]{3,2,1,0:T(4,128)(2,1)S(1)} fusion(bf16[16,192,4,80]{3,2,1,0:T(4,128)(2,1)} %get-tuple-element.232, s32[1024]{0:T(1024)S(1)} %pad_clamp_fusion.2), kind=kCustom, calls=%fused_computation.clone.1 | custom fusion | bytes 983056 | tf_op jit(solution)/shard_map/while/body/eval_jaxpr/gather | solution.py:111
  90.5 1.1 copy_dynamic-update-slice_fusion.2
  91.5 0.6 bitcast_dynamic-update-slice_fusion.3
  92.1 0.6 dynamic_slice.26
  93.4 1.3 constant_dynamic-slice_fusion.2
  94.7 3.1 %gather_fusion = bf16[4,192,4,80]{3,2,1,0:T(4,128)(2,1)S(1)} fusion(bf16[16,192,4,80]{3,2,1,0:T(4,128)(2,1)} %get-tuple-element.234, s32[1024]{0:T(1024)S(1)} %pad_clamp_fusion.2), kind=kCustom, calls=%fused_computation.1.clone.1 | custom fusion | bytes 983056 | tf_op jit(solution)/shard_map/while/body/eval_jaxpr/gather | solution.py:111
  98.2 3.1 %gather_fusion.1 = bf16[4,192,4,80]{3,2,1,0:T(4,128)(2,1)S(1)} fusion(bf16[16,192,4,80]{3,2,1,0:T(4,128)(2,1)} %get-tuple-element.232, s32[1024]{0:T(1024)S(1)} %pad_clamp_fusion.2), kind=kCustom, calls=%fused_computation.clone.1 | custom fusion | bytes 983056 | tf_op jit(solution)/shard_map/while/body/eval_jaxpr/gather | solution.py:111
  102.1 1.0 copy_dynamic-update-slice_fusion.2
  103.2 0.6 bitcast_dynamic-update-slice_fusion.3
  103.8 9.6 %all_to_all.27 = bf16[8,256,4]{1,2,0:T(4,128)(2,1)S(1)} all-to-all(bf16[8,256,4]{1,2,0:T(4,128)(2,1)S(1)} %bitcast.109), channel_id=1, replica_groups=mesh['req'=8,'tp'=4] {'req'}, dimensions={0} | all-to-all | bytes 32768 | tf_op jit(solution)/shard_map/all_to_all | solution.py:119
  113.4 3.3 %all-to-all-start.1 = ((bf16[8,256,4]{1,2,0:T(4,128)(2,1)}), bf16[8,256,4]{1,2,0:T(4,128)(2,1)S(1)}, u32[]{:S(2)}, u32[]{:S(2)}) async-start(bf16[8,256,4]{1,2,0:T(4,128)(2,1)} %bitcast.23), calls=%async_computation.1 | async-start | bytes 32768 | tf_op jit(solution)/shard_map/all_to_all | solution.py:120
  116.7 2.8 %all_to_all.22 = bf16[8,256,320]{1,0,2:T(8,128)(2,1)S(1)} reshape(bf16[4,4,128,4,80]{2,1,0,4,3:T(4,128)(2,1)} %get-tuple-element.68) | data formatting | bytes 2621440 | tf_op jit(solution)/shard_map/all_to_all | solution.py:118
  119.5 1.3 copy.79
  120.8 2.4 %all-to-all-done.1 = bf16[8,256,4]{1,2,0:T(4,128)(2,1)S(1)} async-done(((bf16[8,256,4]{1,2,0:T(4,128)(2,1)}), bf16[8,256,4]{1,2,0:T(4,128)(2,1)S(1)}, u32[]{:S(2)}, u32[]{:S(2)}) %all-to-all-start.1) | async-done | bytes 16416 | tf_op jit(solution)/shard_map/all_to_all | solution.py:120
  123.2 3.7 %all-to-all-start.2 = ((bf16[8,256,320]{1,2,0:T(8,128)(2,1)}), bf16[8,256,320]{1,2,0:T(8,128)(2,1)S(1)}, u32[]{:S(2)}, u32[]{:S(2)}) async-start(bf16[8,256,320]{1,2,0:T(8,128)(2,1)} %copy.79), calls=%async_computation.2 | async-start | bytes 2621440 | tf_op jit(solution)/shard_map/all_to_all | solution.py:118
  127.0 1.6 convolution_convert_fusion
  128.7 1.6 convolution_convert_fusion.2
  131.1 25.4 %all-to-all-done.2 = bf16[8,256,320]{1,2,0:T(8,128)(2,1)S(1)} async-done(((bf16[8,256,320]{1,2,0:T(8,128)(2,1)}), bf16[8,256,320]{1,2,0:T(8,128)(2,1)S(1)}, u32[]{:S(2)}, u32[]{:S(2)}) %all-to-all-start.2) | async-done | bytes 1310752 | tf_op jit(solution)/shard_map/all_to_all | solution.py:118
  156.9 1.6 fusion.55
  158.6 38.0 %all-reduce.2.cloned.1.call-done = f32[256,1280]{0,1:T(8,128)} async-done(((f32[256,1280]{0,1:T(8,128)}), f32[256,1280]{0,1:T(8,128)}) %all-reduce.2.cloned.1.call-update) | async-done | bytes 1310736 | tf_op jit(solution)/shard_map/psum | solution.py:139
  196.6 1.6 fusion.10
  198.2 3.6 %convolution_bitcast_fusion.1 = f32[1280,256]{1,0:T(8,128)} fusion(bf16[320,1280]{1,0:T(8,128)(2,1)S(1)} %copy-done.7, bf16[1280,320]{0,1:T(8,128)(2,1)} %param.24, bf16[256,1280]{0,1:T(8,128)(2,1)S(1)} %get-tuple-element.124, f32[1280]{0:T(1024)S(1)} %convert_element_type.81, f32[256]{0:T(256)S(1)} %add_rsqrt_fusion), kind=kOutput, calls=%fused_computation.20 | convolution fusion | flops 421150720 | bytes 3610624
  201.7 0.6 copy-done.9
  203.0 1.2 compare_select_fusion.2
  204.3 24.2 %reduce-scatter.4.cloned.1.call-done = f32[320,256]{1,0:T(8,128)} async-done(((f32[1280,256]{1,0:T(8,128)}), f32[320,256]{1,0:T(8,128)}) %reduce-scatter.4.cloned.1.call-update) | async-done | bytes 327696
  228.5 1.7 fusion.28
  (78 shorter events, 8.4 us)
Async XLA Ops:
  6.5 150.3 %copy-start = (bf16[320,1280]{1,0:T(8,128)(2,1)S(1)}, bf16[320,1280]{1,0:T(8,128)(2,1)}, u32[]{:S(2)}) copy-start(bf16[320,1280]{1,0:T(8,128)(2,1)} %param.23) | copy-start | bytes 2457604
  6.5 1.5 copy-start.4
  6.5 1.7 copy-start.6
  6.5 48.0 %all-gather.2.cloned.1.call-start = ((), (), s32[]{:S(2)}) async-start(), calls=%async_computation.4 | async-start | bytes 1474560 | tf_op jit(solution)/shard_map/all_gather | solution.py:103
  8.0 1.4 copy-start.1
  54.6 2.7 %copy-start.8 = (s32[16]{0:T(128)S(1)}, s32[16]{0:T(128)}, u32[]{:S(2)}) copy-start(s32[16]{0:T(128)} %param.28) | copy-start | bytes 196
  113.4 9.8 %all-to-all-start.1 = ((bf16[8,256,4]{1,2,0:T(4,128)(2,1)}), bf16[8,256,4]{1,2,0:T(4,128)(2,1)S(1)}, u32[]{:S(2)}, u32[]{:S(2)}) async-start(bf16[8,256,4]{1,2,0:T(4,128)(2,1)} %bitcast.23), calls=%async_computation.1 | async-start | bytes 32768 | tf_op jit(solution)/shard_map/all_to_all | solution.py:120
  120.8 6.1 %copy-start.3 = (bf16[256,320]{0,1:T(8,128)(2,1)S(1)}, bf16[256,320]{0,1:T(8,128)(2,1)}, u32[]{:S(2)}) copy-start(bf16[256,320]{0,1:T(8,128)(2,1)} %convolution_convert_fusion.1) | copy-start | bytes 491524
  120.8 6.2 %copy-start.2 = (bf16[256,1280]{0,1:T(8,128)(2,1)S(1)}, bf16[256,1280]{0,1:T(8,128)(2,1)}, u32[]{:S(2)}) copy-start(bf16[256,1280]{0,1:T(8,128)(2,1)} %copy-done.1) | copy-start | bytes 1966084
  123.2 33.3 %all-to-all-start.2 = ((bf16[8,256,320]{1,2,0:T(8,128)(2,1)}), bf16[8,256,320]{1,2,0:T(8,128)(2,1)S(1)}, u32[]{:S(2)}, u32[]{:S(2)}) async-start(bf16[8,256,320]{1,2,0:T(8,128)(2,1)} %copy.79), calls=%async_computation.2 | async-start | bytes 2621440 | tf_op jit(solution)/shard_map/all_to_all | solution.py:118
  126.9 69.7 %all-reduce.2.cloned.1.call-start = ((), (), s32[]{:S(2)}) async-start(), calls=%async_computation.5 | async-start | bytes 2621440 | tf_op jit(solution)/shard_map/psum | solution.py:139
  156.8 1.7 copy-start.5
  158.5 70.0 %reduce-scatter.4.cloned.1.call-start = ((), (), s32[]{:S(2)}) async-start(), calls=%async_computation.6 | async-start | bytes 1638400
  158.6 39.6 %copy-start.7 = (bf16[320,1280]{1,0:T(8,128)(2,1)S(1)}, bf16[320,1280]{1,0:T(8,128)(2,1)}, u32[]{:S(2)}) copy-start(bf16[320,1280]{1,0:T(8,128)(2,1)} %param.25) | copy-start | bytes 2457604
  201.7 0.7 copy-start.9
Sparse Core Ops, SparseCore 0:
  9.6 44.9 all-gather.1
  158.6 37.8 all-reduce.1
  201.9 26.5 reduce-scatter.3
where the time goes:
time: 238 us; the launch traced here: 237 us
  waiting for transfers between devices  121 us (51%)
  local copies, waits for them, and re-layouts  60.8 us (26%)
  matrix products  13.8 us (6%)
  between operations  13.4 us (6%)
  blocking collectives  9.64 us (4%)
  other arithmetic  8.89 us (4%)
  starting transfers between devices  7.01 us (3%)
  loops' own time  2.73 us (1%)
    psum x1, waiting for transfers between devices, per_device(): summed = lax.psum(head_terms, 'tp')  38 us
    all_gather x1, waiting for transfers between devices, per_device(): gathered = lax.all_gather(queries, 'req', axis=0, tiled=True)  30.5 us
    all_to_all x1, waiting for transfers between devices, per_device(): lax.all_to_all(shares, 'req', split_axis=0, concat_axis=0, tiled=True)  25.4 us
    unnamed x4, waiting for transfers between devices  24.3 us
    gather x4, local copies, waits for them, and re-layouts, padded_block(): prefix_values[chosen]  12.4 us
    gather x4, local copies, waits for them, and re-layouts, padded_block(): prefix_keys[chosen]  12.4 us
    unnamed x24, local copies, waits for them, and re-layouts  10.9 us
    all_to_all x1, blocking collectives, per_device(): lax.all_to_all(maxima, 'req', split_axis=0, concat_axis=0, tiled=True)  9.64 us
  transfers between devices with their start and end apart: 5, of which 5 were waited for; matrix products, arithmetic and copies ran while one was open for 9% of the time, Pallas kernels for 0%

commit v1 on v0

v1 whole, which is shorter than its diff:
```python
import functools
import math

import jax
import jax.numpy as jnp
from jax import lax
from jax.experimental import pallas as pl
from jax.experimental.pallas import tpu as pltpu
from jax.sharding import PartitionSpec as P

HDIM = 80
SLOT = 128
R_DEV = 2
PG = 192
LOCAL_HEADS = 4
WIDTH = HDIM * LOCAL_HEADS
ROWS = R_DEV * SLOT
STATS = 16
HALF = WIDTH // 2

EPSILON = 1e-06
NEGATIVE = -1e30
MESH = pl.DeviceIdType.MESH
F32 = jnp.float32
BF16 = jnp.bfloat16


def normalize(floats, gain):
    mean_square = jnp.mean(floats * floats, axis=-1, keepdims=True)
    return (floats * lax.rsqrt(mean_square + EPSILON) * gain).astype(BF16)


def matmul(left, right):
    return jnp.dot(left, right, preferred_element_type=F32)


def head_rows(values, head):
    return values[head * HDIM : (head + 1) * HDIM]


def request_partial(query_t, keys, values_t, causal):
    none = jnp.zeros((HDIM, SLOT), BF16)
    spread = jnp.concatenate(
        [
            jnp.concatenate(
                [head_rows(query_t, h) if g == h else none for g in range(LOCAL_HEADS)], axis=1
            )
            for h in range(LOCAL_HEADS)
        ],
        axis=0,
    )
    scores = matmul(keys, spread) * (1.0 / math.sqrt(HDIM))
    if causal:
        key_row = lax.broadcasted_iota(jnp.int32, scores.shape, 0)
        query_row = lax.broadcasted_iota(jnp.int32, scores.shape, 1) % SLOT
        scores = jnp.where(key_row <= query_row, scores, NEGATIVE)
    top = jnp.max(scores, axis=0, keepdims=True)
    if not causal:
        top = top.astype(BF16).astype(F32)
    weights = jnp.exp(scores - top)
    total = jnp.sum(weights, axis=0, keepdims=True)
    numer = matmul(values_t, weights.astype(BF16))
    lanes = [slice(h * SLOT, (h + 1) * SLOT) for h in range(LOCAL_HEADS)]
    return [(head_rows(numer, h)[:, lanes[h]], top[:, lanes[h]], total[:, lanes[h]]) for h in range(LOCAL_HEADS)]


def both_requests(first, second):
    return [
        tuple(jnp.concatenate([a, b], axis=1) for a, b in zip(first[h], second[h]))
        for h in range(LOCAL_HEADS)
    ]


def merge(one, other):
    merged = []
    for (numer_a, top_a, total_a), (numer_b, top_b, total_b) in zip(one, other):
        top = jnp.maximum(top_a, top_b)
        factor_a = jnp.exp(top_a - top)
        factor_b = jnp.exp(top_b - top)
        merged.append(
            (
                numer_a * factor_a + numer_b * factor_b,
                top,
                total_a * factor_a + total_b * factor_b,
            )
        )
    return merged


def pack_partial(partial):
    shares = [(numer / total).astype(BF16) for numer, _, total in partial]
    tops = [top for _, top, _ in partial]
    whole = [total.astype(BF16).astype(F32) for _, _, total in partial]
    rest = [total - high for (_, _, total), high in zip(partial, whole)]
    pad = [jnp.zeros((STATS - 3 * LOCAL_HEADS, ROWS), F32)]
    stats = jnp.concatenate(tops + whole + rest + pad, axis=0).astype(BF16)
    return jnp.concatenate(shares + [stats], axis=0)


def unpack_partial(block):
    stats = block[WIDTH:].astype(F32)
    partial = []
    for h in range(LOCAL_HEADS):
        top = stats[h : h + 1]
        total = stats[LOCAL_HEADS + h : LOCAL_HEADS + h + 1]
        total = total + stats[2 * LOCAL_HEADS + h : 2 * LOCAL_HEADS + h + 1]
        partial.append((head_rows(block, h).astype(F32) * total, top, total))
    return partial


def kernel(
    nz,
    tokens,
    gain_a,
    gain_f,
    wq,
    wk,
    wv,
    wo,
    wup,
    wdown,
    cache_k,
    cache_v,
    prefix,
    length,
    out,
    qbuf,
    kbuf,
    vbuf,
    wo_all,
    up_v,
    down_v,
    down_t,
    own_k,
    own_v,
    upward,
    downward,
    cross,
    att,
    core_out,
    core_in,
    y_out,
    y_in,
    mid_t,
    local_sem,
    qsend,
    qrecv,
    psend,
    precv,
    xsend,
    xrecv,
    tsend,
    trecv,
):
    me = lax.axis_index("req")
    tp = lax.axis_index("tp")
    z = me // 2
    x = me % 2
    mate = z * 2 + 1 - x
    core_mate = tp + 1 - 2 * (tp % 2)
    y_mate = (tp + 2) % 4
    not_first = z > 0
    not_last = z < nz - 1

    def remote(source, target, send_sem, recv_sem, **where):
        return pltpu.make_async_remote_copy(
            src_ref=source,
            dst_ref=target,
            send_sem=send_sem,
            recv_sem=recv_sem,
            device_id=where,
            device_id_type=MESH,
        )

    barrier = pltpu.get_barrier_semaphore()

    def greet(**where):
        pl.semaphore_signal(barrier, inc=1, device_id=where, device_id_type=MESH)

    greet(req=mate)
    greet(tp=core_mate)
    greet(tp=y_mate)
    pl.when(not_first)(lambda: greet(req=me - 2))
    pl.when(not_last)(lambda: greet(req=me + 2))

    loads = [
        pltpu.make_async_copy(source, target, local_sem.at[i])
        for i, (source, target) in enumerate(
            [(wo, wo_all.at[tp]), (cache_k, kbuf), (cache_v, vbuf), (wdown, down_v), (wup, up_v)]
        )
    ]
    for load in loads:
        load.start()

    normed = normalize(tokens[...].astype(F32), gain_a[...].astype(F32))
    qbuf[me] = matmul(normed, wq[...]).T.astype(BF16)

    pl.semaphore_wait(barrier, 3 + jnp.where(not_first, 1, 0) + jnp.where(not_last, 1, 0))

    def whole(plane, column):
        return qbuf.at[plane * 2 + column]

    def early(plane, column):
        return qbuf.at[plane * 2 + column, pl.ds(0, HALF)]

    def late(plane, column):
        return qbuf.at[plane * 2 + column, pl.ds(HALF, HALF)]

    def up_whole(plane):
        return remote(whole(plane, x), whole(plane, x), qsend.at[0, plane], qrecv.at[0, plane], req=me + 2)

    def up_early(plane):
        return remote(early(plane, 1 - x), early(plane, 1 - x), qsend.at[1, plane], qrecv.at[1, plane], req=me + 2)

    def down_whole(plane):
        return remote(whole(plane, x), whole(plane, x), qsend.at[2, plane], qrecv.at[0, plane], req=me - 2)

    def down_early(plane):
        return remote(early(plane, 1 - x), early(plane, 1 - x), qsend.at[3, plane], qrecv.at[1, plane], req=me - 2)

    def over_late(plane):
        return remote(late(plane, x), late(plane, x), qsend.at[4, plane], qrecv.at[2, plane], req=mate)

    over_whole = remote(whole(z, x), whole(z, x), qsend.at[4, z], qrecv.at[2, z], req=mate)
    got_whole = remote(whole(z, 1 - x), whole(z, 1 - x), qsend.at[4, z], qrecv.at[2, z], req=mate)

    over_whole.start()
    pl.when(not_last)(lambda: up_whole(z).start())
    pl.when(not_first)(lambda: down_whole(z).start())

    loads[0].wait()
    wo_y = remote(wo_all.at[tp], wo_all.at[tp], tsend.at[0], trecv.at[0], tp=y_mate)
    wo_core = remote(wo_all.at[tp], wo_all.at[tp], tsend.at[1], trecv.at[1], tp=core_mate)
    wo_y.start()
    wo_core.start()

    got_whole.wait_recv()
    pl.when(not_last)(lambda: up_early(z).start())
    pl.when(not_first)(lambda: down_early(z).start())

    own_k[...] = matmul(normed, wk[...]).astype(BF16)
    own_v[...] = matmul(normed, wv[...]).T.astype(BF16)
    loads[3].wait()
    down_t[...] = down_v[...].astype(F32).T.astype(BF16)

    def gather_step(step, carry):
        below = z - 1 - step
        above = z + 1 + step

        @pl.when(below >= 0)
        def _():
            up_whole(below).wait_recv()
            pl.when(not_last)(lambda: up_whole(below).start())
            over_late(below).start()

        @pl.when(above < nz)
        def _():
            down_whole(above).wait_recv()
            pl.when(not_first)(lambda: down_whole(above).start())
            over_late(above).start()

        @pl.when(below >= 0)
        def _():
            up_early(below).wait_recv()
            pl.when(not_last)(lambda: up_early(below).start())

        @pl.when(above < nz)
        def _():
            down_early(above).wait_recv()
            pl.when(not_first)(lambda: down_early(above).start())

        return carry

    lax.fori_loop(0, nz - 1, gather_step, 0)

    def late_step(plane, carry):
        @pl.when(plane != z)
        def _():
            remote(late(plane, 1 - x), late(plane, 1 - x), qsend.at[4, plane], qrecv.at[2, plane], req=mate).wait_recv()

        return carry

    lax.fori_loop(0, nz, late_step, 0)
    loads[1].wait()
    loads[2].wait()

    def cached(target):
        queries = qbuf[target]
        parts = []
        for j in range(R_DEV):
            chosen = prefix[target * R_DEV + j]
            parts.append(
                request_partial(
                    queries[:, j * SLOT : (j + 1) * SLOT],
                    kbuf[chosen],
                    vbuf[chosen].astype(F32).T.astype(BF16),
                    False,
                )
            )
        return both_requests(*parts)

    def send_up(slot):
        return remote(upward.at[slot], upward.at[slot], psend.at[0, slot], precv.at[0, slot], req=me + 2)

    def send_down(slot):
        return remote(downward.at[slot], downward.at[slot], psend.at[1, slot], precv.at[1, slot], req=me - 2)

    def climb(slot):
        upward[slot] = pack_partial(cached(slot))

    def climb_merged(slot):
        own = cached(slot)
        send_up(slot).wait_recv()
        upward[slot] = pack_partial(merge(own, unpack_partial(upward[slot])))

    def descend(slot):
        downward[slot] = pack_partial(cached(slot))

    def descend_merged(slot):
        own = cached(slot)
        send_down(slot).wait_recv()
        downward[slot] = pack_partial(merge(own, unpack_partial(downward[slot])))

    def return_step(step, carry):
        high = (nz - 1 - step // 2) * 2 + step % 2
        low = step

        @pl.when(high // 2 > z)
        def _():
            pl.when(not_first)(lambda: climb_merged(high))
            pl.when(z == 0)(lambda: climb(high))
            send_up(high).start()

        @pl.when(low // 2 < z)
        def _():
            pl.when(not_last)(lambda: descend_merged(low))
            pl.when(z == nz - 1)(lambda: descend(low))
            send_down(low).start()

        return carry

    lax.fori_loop(0, (nz - 1) * 2, return_step, 0)

    own = both_requests(
        *[
            request_partial(
                qbuf[me, :, pl.ds(j * SLOT, SLOT)],
                own_k[pl.ds(j * SLOT, SLOT), :],
                own_v[:, pl.ds(j * SLOT, SLOT)],
                True,
            )
            for j in range(R_DEV)
        ]
    )
    mine = merge(own, cached(me))

    cross[0] = pack_partial(cached(mate))

    @pl.when(not_first)
    def _():
        send_up(mate).wait_recv()
        cross[0] = pack_partial(merge(unpack_partial(cross[0]), unpack_partial(upward[mate])))

    @pl.when(not_last)
    def _():
        send_down(mate).wait_recv()
        cross[0] = pack_partial(merge(unpack_partial(cross[0]), unpack_partial(downward[mate])))

    to_mate = remote(cross.at[0], cross.at[1], xsend, xrecv, req=mate)
    to_mate.start()

    remote(wo_all.at[y_mate], wo_all.at[y_mate], tsend.at[0], trecv.at[0], tp=y_mate).wait_recv()
    wo_far = remote(wo_all.at[y_mate], wo_all.at[y_mate], tsend.at[2], trecv.at[2], tp=core_mate)
    wo_far.start()

    nothing = [(jnp.zeros((HDIM, ROWS), F32), jnp.full((1, ROWS), NEGATIVE, F32), jnp.zeros((1, ROWS), F32))] * LOCAL_HEADS

    @pl.when(z == 0)
    def _():
        upward[me] = jnp.zeros(upward.shape[1:], BF16)

    @pl.when(not_first)
    def _():
        send_up(me).wait_recv()

    @pl.when(z == nz - 1)
    def _():
        downward[me] = jnp.zeros(downward.shape[1:], BF16)

    @pl.when(not_last)
    def _():
        send_down(me).wait_recv()

    def present(condition, partial):
        return [
            (numer, jnp.where(condition, top, empty), total)
            for (numer, top, total), (_, empty, _) in zip(partial, nothing)
        ]

    mine = merge(mine, present(not_first, unpack_partial(upward[me])))
    mine = merge(mine, present(not_last, unpack_partial(downward[me])))
    to_mate.wait_recv()
    mine = merge(mine, unpack_partial(cross[1]))
    att[tp] = jnp.concatenate([(numer / total).astype(BF16) for numer, _, total in mine], axis=0)

    att_y = remote(att.at[tp], att.at[tp], tsend.at[3], trecv.at[3], tp=y_mate)
    att_core = remote(att.at[tp], att.at[tp], tsend.at[4], trecv.at[4], tp=core_mate)
    att_y.start()
    att_core.start()

    def projected(index):
        return matmul(att[index].astype(F32).T.astype(BF16), wo_all[index])

    terms = projected(tp)
    remote(wo_all.at[core_mate], wo_all.at[core_mate], tsend.at[1], trecv.at[1], tp=core_mate).wait_recv()
    remote(att.at[core_mate], att.at[core_mate], tsend.at[4], trecv.at[4], tp=core_mate).wait_recv()
    terms = terms + projected(core_mate)
    remote(att.at[y_mate], att.at[y_mate], tsend.at[3], trecv.at[3], tp=y_mate).wait_recv()
    att_far = remote(att.at[y_mate], att.at[y_mate], tsend.at[5], trecv.at[5], tp=core_mate)
    att_far.start()
    terms = terms + projected(y_mate)
    diagonal = (core_mate + 2) % 4
    remote(wo_all.at[diagonal], wo_all.at[diagonal], tsend.at[2], trecv.at[2], tp=core_mate).wait_recv()
    remote(att.at[diagonal], att.at[diagonal], tsend.at[5], trecv.at[5], tp=core_mate).wait_recv()
    terms = terms + projected(diagonal)

    middle = (tokens[...].astype(F32) + terms).astype(BF16).astype(F32)
    normed_middle = normalize(middle, gain_f[...].astype(F32))
    loads[4].wait()
    gate = matmul(normed_middle, up_v[...])
    hidden_t = (gate / (1.0 + jnp.exp(-gate))).T.astype(BF16)

    def down_part(index):
        return matmul(down_t[pl.ds(pl.multiple_of(index * WIDTH, 16), WIDTH)], hidden_t)

    core_out[0] = down_part(diagonal).astype(BF16)
    core_out[1] = down_part(core_mate).astype(BF16)
    fold = remote(core_out, core_in, tsend.at[6], trecv.at[6], tp=core_mate)
    fold.start()
    far_part = down_part(y_mate)
    near_part = down_part(tp)
    mid_t[...] = middle.T
    near_part = near_part + mid_t[pl.ds(pl.multiple_of(tp * WIDTH, 16), WIDTH)]
    fold.wait_recv()
    y_out[...] = (far_part + core_in[0].astype(F32)).astype(BF16)
    swap = remote(y_out, y_in, tsend.at[7], trecv.at[7], tp=y_mate)
    swap.start()
    near_part = near_part + core_in[1].astype(F32)
    lane = lax.broadcasted_iota(jnp.int32, (WIDTH, ROWS), 1)
    live = jnp.where(lane < SLOT, length[me * R_DEV], length[me * R_DEV + 1])
    swap.wait_recv()
    layer = near_part + y_in[...].astype(F32)
    out[...] = jnp.where(lane % SLOT < live, layer, 0.0).T.astype(BF16)

    over_whole.wait_send()

    def sent_step(plane, carry):
        pl.when(plane != z)(lambda: over_late(plane).wait_send())

        @pl.when(jnp.logical_and(not_last, plane <= z))
        def _():
            up_whole(plane).wait_send()
            up_early(plane).wait_send()

        @pl.when(jnp.logical_and(not_first, plane >= z))
        def _():
            down_whole(plane).wait_send()
            down_early(plane).wait_send()

        for column in range(2):
            slot = plane * 2 + column
            pl.when(plane > z)(lambda: send_up(slot).wait_send())
            pl.when(plane < z)(lambda: send_down(slot).wait_send())
        return carry

    lax.fori_loop(0, nz, sent_step, 0)
    for copy in (to_mate, wo_y, wo_core, wo_far, att_y, att_core, att_far, fold, swap):
        copy.wait_send()


def per_device(
    tokens,
    attention_gain,
    feedforward_gain,
    query_weight,
    key_weight,
    value_weight,
    out_weight,
    up_weight,
    down_weight,
    cache_keys,
    cache_values,
    request_prefix,
    suffix_length,
):
    owners = lax.axis_size("req")
    nz = owners // 2
    rows, model = tokens.shape
    prefixes = cache_keys.shape[1]
    dma = pltpu.SemaphoreType.DMA
    vmem = pl.BlockSpec(memory_space=pltpu.VMEM)
    smem = pl.BlockSpec(memory_space=pltpu.SMEM)
    away = pl.BlockSpec(memory_space=pl.ANY)
    return pl.pallas_call(
        functools.partial(kernel, nz),
        out_shape=jax.ShapeDtypeStruct((rows, WIDTH), BF16),
        in_specs=[vmem] * 6 + [away] * 5 + [smem] * 2,
        out_specs=vmem,
        scratch_shapes=[
            pltpu.VMEM((owners, WIDTH, ROWS), BF16),
            pltpu.VMEM((prefixes, PG, WIDTH), BF16),
            pltpu.VMEM((prefixes, PG, WIDTH), BF16),
            pltpu.VMEM((4, WIDTH, model), BF16),
            pltpu.VMEM((model, WIDTH), BF16),
            pltpu.VMEM((WIDTH, model), BF16),
            pltpu.VMEM((model, WIDTH), BF16),
            pltpu.VMEM((ROWS, WIDTH), BF16),
            pltpu.VMEM((WIDTH, ROWS), BF16),
            pltpu.VMEM((owners, WIDTH + STATS, ROWS), BF16),
            pltpu.VMEM((owners, WIDTH + STATS, ROWS), BF16),
            pltpu.VMEM((2, WIDTH + STATS, ROWS), BF16),
            pltpu.VMEM((4, WIDTH, ROWS), BF16),
            pltpu.VMEM((2, WIDTH, ROWS), BF16),
            pltpu.VMEM((2, WIDTH, ROWS), BF16),
            pltpu.VMEM((WIDTH, ROWS), BF16),
            pltpu.VMEM((WIDTH, ROWS), BF16),
            pltpu.VMEM((model, ROWS), F32),
            dma((5,)),
            dma((5, nz)),
            dma((3, nz)),
            dma((2, owners)),
            dma((2, owners)),
            dma,
            dma,
            dma((8,)),
            dma((8,)),
        ],
        compiler_params=pltpu.CompilerParams(
            collective_id=0, has_side_effects=True, vmem_limit_bytes=60 * 1024 * 1024
        ),
    )(
        tokens,
        attention_gain.reshape(1, model),
        feedforward_gain.reshape(1, model),
        query_weight,
        key_weight,
        value_weight,
        out_weight,
        up_weight,
        down_weight,
        cache_keys[0],
        cache_values[0],
        request_prefix,
        suffix_length,
    )


def solution(mesh):
    in_specs = (
        P("req", None),
        P(),
        P(),
        P(None, "tp"),
        P(None, "tp"),
        P(None, "tp"),
        P("tp", None),
        P(None, "tp"),
        P("tp", None),
        P("req", None, None, "tp"),
        P("req", None, None, "tp"),
        P(),
        P(),
    )
    out_specs = P("req", "tp")
    return jax.shard_map(
        per_device, mesh=mesh, in_specs=in_specs, out_specs=out_specs, check_vma=False
    )
```

time: 238 us -> 90.7 us (0.38)
  the two profiles are of different devices: /device:TPU:0 before, /device:TPU:18 now
where the time goes in v1:
time: 90.7 us; the launch traced here: 90.5 us
  Pallas kernels  79.9 us (88%)
  local copies, waits for them, and re-layouts  10.6 us (12%)
    pallas_call x1, Pallas kernels, per_device(): pl.pallas_call(functools.partial(kernel, nz), out_shape=jax.ShapeDtypeStr...  79.9 us
    unnamed x10, local copies, waits for them, and re-layouts  6.21 us

profile of v1, /device:TPU:18, one launch (start us, length us, event | category | flops | bytes accessed | tf_op | source)
XLA Modules:
  0.0 90.5 jit_solution(3438894561071518712)
XLA Ops:
  0.0 0.0 copy-start.1
  0.0 0.0 copy-start
  0.0 1.4 %reshape.6.gain_a = bf16[1,1280]{1,0:T(2,128)(2,1)} reshape(bf16[1280]{0:T(1024)(128)(2,1)} %param.14) | data formatting | bytes 5120 | tf_op jit(solution)/shard_map/reshape | solution.py:543
  1.4 1.3 %reshape.7.gain_f = bf16[1,1280]{1,0:T(2,128)(2,1)} reshape(bf16[1280]{0:T(1024)(128)(2,1)} %param.15) | data formatting | bytes 5120 | tf_op jit(solution)/shard_map/reshape | solution.py:544
  2.7 0.0 copy-start.2
  2.7 2.3 %copy.14.wq = bf16[1280,320]{1,0:T(8,128)(2,1)} copy(bf16[1280,320]{0,1:T(8,128)(2,1)} %param.16) | data formatting | bytes 1638400 | tf_op args[3]
  5.0 0.0 copy-done
  5.0 1.3 %copy.15.wk = bf16[1280,320]{1,0:T(8,128)(2,1)} copy(bf16[1280,320]{0,1:T(8,128)(2,1)S(1)} %copy-done) | data formatting | bytes 1638400 | tf_op args[4]
  6.3 0.0 copy-done.1
  6.3 1.3 %copy.16.wv = bf16[1280,320]{1,0:T(8,128)(2,1)} copy(bf16[1280,320]{0,1:T(8,128)(2,1)S(1)} %copy-done.1) | data formatting | bytes 1638400 | tf_op args[5]
  7.6 0.0 copy-done.2
  7.6 1.3 %copy.17.wup = bf16[1280,320]{1,0:T(8,128)(2,1)} copy(bf16[1280,320]{0,1:T(8,128)(2,1)S(1)} %copy-done.2) | data formatting | bytes 1638400 | tf_op args[7]
  8.9 79.9 %shard_map.127 = bf16[256,320]{1,0:T(8,128)(2,1)} custom-call(bf16[256,1280]{1,0:T(8,128)(2,1)} %tokens.1, bf16[1,1280]{1,0:T(2,128)(2,1)} %reshape.6.gain_a, bf16[1,1280]{1,0:T(2,128)(2,1)} %reshape.7.gain_f, bf16[1280,320]{1,0:T(8,128)(2,1)} %copy.14.wq, bf16[1280,320]{1,0:T(8,128)(2,1)} %copy.15.wk, bf16[1280,320]{1,0:T(8,128)(2,1)} %copy.16.wv, ...), custom_call_target="tpu_custom_call" | custom-call | tf_op jit(solution)/shard_map/pallas_call | solution.py:504
  88.8 1.7 %copy.18 = bf16[256,320]{0,1:T(8,128)(2,1)} copy(bf16[256,320]{1,0:T(8,128)(2,1)} %shard_map.127) | data formatting | bytes 327680 | tf_op jit(solution)/shard_map/pallas_call | solution.py:504
Async XLA Ops:
  0.0 6.3 %copy-start.1 = (bf16[1280,320]{0,1:T(8,128)(2,1)S(1)}, bf16[1280,320]{0,1:T(8,128)(2,1)}, u32[]{:S(2)}) copy-start(bf16[1280,320]{0,1:T(8,128)(2,1)} %param.18) | copy-start | bytes 2457604
  0.0 5.0 %copy-start = (bf16[1280,320]{0,1:T(8,128)(2,1)S(1)}, bf16[1280,320]{0,1:T(8,128)(2,1)}, u32[]{:S(2)}) copy-start(bf16[1280,320]{0,1:T(8,128)(2,1)} %param.17) | copy-start | bytes 2457604
  2.7 4.9 %copy-start.2 = (bf16[1280,320]{0,1:T(8,128)(2,1)S(1)}, bf16[1280,320]{0,1:T(8,128)(2,1)}, u32[]{:S(2)}) copy-start(bf16[1280,320]{0,1:T(8,128)(2,1)} %param.20) | copy-start | bytes 2457604

commit v2 on v1

--- a/solution.py
+++ b/solution.py
@@ -32,6 +32,10 @@
 
 def matmul(left, right):
     return jnp.dot(left, right, preferred_element_type=F32)
+
+
+def matmul_rows(left, right):
+    return lax.dot_general(left, right, (((1,), (1,)), ((), ())), preferred_element_type=F32)
 
 
 def head_rows(values, head):
@@ -88,22 +92,24 @@
 
 
 def pack_partial(partial):
+    heads = len(partial)
     shares = [(numer / total).astype(BF16) for numer, _, total in partial]
     tops = [top for _, top, _ in partial]
     whole = [total.astype(BF16).astype(F32) for _, _, total in partial]
     rest = [total - high for (_, _, total), high in zip(partial, whole)]
-    pad = [jnp.zeros((STATS - 3 * LOCAL_HEADS, ROWS), F32)]
+    pad = [jnp.zeros((STATS - 3 * heads, ROWS), F32)]
     stats = jnp.concatenate(tops + whole + rest + pad, axis=0).astype(BF16)
     return jnp.concatenate(shares + [stats], axis=0)
 
 
 def unpack_partial(block):
-    stats = block[WIDTH:].astype(F32)
+    heads = (block.shape[0] - STATS) // HDIM
+    stats = block[heads * HDIM :].astype(F32)
     partial = []
-    for h in range(LOCAL_HEADS):
+    for h in range(heads):
         top = stats[h : h + 1]
-        total = stats[LOCAL_HEADS + h : LOCAL_HEADS + h + 1]
-        total = total + stats[2 * LOCAL_HEADS + h : 2 * LOCAL_HEADS + h + 1]
+        total = stats[heads + h : heads + h + 1]
+        total = total + stats[2 * heads + h : 2 * heads + h + 1]
         partial.append((head_rows(block, h).astype(F32) * total, top, total))
     return partial
 
@@ -133,8 +139,12 @@
     down_t,
     own_k,
     own_v,
-    upward,
-    downward,
+    cache_vt,
+    numers,
+    stats,
+    full_way,
+    half_way,
+    over,
     cross,
     att,
     core_out,
@@ -151,6 +161,8 @@
     xrecv,
     tsend,
     trecv,
+    osend,
+    orecv,
 ):
     me = lax.axis_index("req")
     tp = lax.axis_index("tp")
@@ -192,8 +204,8 @@
     for load in loads:
         load.start()
 
-    normed = normalize(tokens[...].astype(F32), gain_a[...].astype(F32))
-    qbuf[me] = matmul(normed, wq[...]).T.astype(BF16)
+    normed = normalize(tokens[...].astype(F32), gain_a[...].astype(F32)[None, :])
+    qbuf[me] = matmul_rows(wq[...], normed).astype(BF16)
 
     pl.semaphore_wait(barrier, 3 + jnp.where(not_first, 1, 0) + jnp.where(not_last, 1, 0))
 
@@ -238,51 +250,25 @@
     pl.when(not_last)(lambda: up_early(z).start())
     pl.when(not_first)(lambda: down_early(z).start())
 
-    own_k[...] = matmul(normed, wk[...]).astype(BF16)
-    own_v[...] = matmul(normed, wv[...]).T.astype(BF16)
-    loads[3].wait()
-    down_t[...] = down_v[...].astype(F32).T.astype(BF16)
-
-    def gather_step(step, carry):
-        below = z - 1 - step
-        above = z + 1 + step
-
-        @pl.when(below >= 0)
-        def _():
-            up_whole(below).wait_recv()
-            pl.when(not_last)(lambda: up_whole(below).start())
-            over_late(below).start()
-
-        @pl.when(above < nz)
-        def _():
-            down_whole(above).wait_recv()
-            pl.when(not_first)(lambda: down_whole(above).start())
-            over_late(above).start()
-
-        @pl.when(below >= 0)
-        def _():
-            up_early(below).wait_recv()
-            pl.when(not_last)(lambda: up_early(below).start())
-
-        @pl.when(above < nz)
-        def _():
-            down_early(above).wait_recv()
-            pl.when(not_first)(lambda: down_early(above).start())
-
-        return carry
-
-    lax.fori_loop(0, nz - 1, gather_step, 0)
-
-    def late_step(plane, carry):
-        @pl.when(plane != z)
-        def _():
-            remote(late(plane, 1 - x), late(plane, 1 - x), qsend.at[4, plane], qrecv.at[2, plane], req=mate).wait_recv()
-
-        return carry
-
-    lax.fori_loop(0, nz, late_step, 0)
-    loads[1].wait()
-    loads[2].wait()
+    own_k[...] = matmul_rows(normed, wk[...]).astype(BF16)
+    own_v[...] = matmul_rows(wv[...], normed).astype(BF16)
+
+    def save(way, column, partial):
+        for h, (numer, top, total) in enumerate(partial):
+            numers[way, column, pl.ds(h * HDIM, HDIM)] = numer
+            stats[way, column, pl.ds(h, 1)] = top
+            stats[way, column, pl.ds(LOCAL_HEADS + h, 1)] = total
+
+    def load(way, column):
+        held = stats[way, column]
+        return [
+            (
+                numers[way, column, pl.ds(h * HDIM, HDIM)],
+                held[h : h + 1],
+                held[LOCAL_HEADS + h : LOCAL_HEADS + h + 1],
+            )
+            for h in range(LOCAL_HEADS)
+        ]
 
     def cached(target):
         queries = qbuf[target]
@@ -291,81 +277,156 @@
             chosen = prefix[target * R_DEV + j]
             parts.append(
                 request_partial(
-                    queries[:, j * SLOT : (j + 1) * SLOT],
-                    kbuf[chosen],
-                    vbuf[chosen].astype(F32).T.astype(BF16),
-                    False,
+                    queries[:, j * SLOT : (j + 1) * SLOT], kbuf[chosen], cache_vt[chosen], False
                 )
             )
         return both_requests(*parts)
 
-    def send_up(slot):
-        return remote(upward.at[slot], upward.at[slot], psend.at[0, slot], precv.at[0, slot], req=me + 2)
-
-    def send_down(slot):
-        return remote(downward.at[slot], downward.at[slot], psend.at[1, slot], precv.at[1, slot], req=me - 2)
-
-    def climb(slot):
-        upward[slot] = pack_partial(cached(slot))
-
-    def climb_merged(slot):
-        own = cached(slot)
-        send_up(slot).wait_recv()
-        upward[slot] = pack_partial(merge(own, unpack_partial(upward[slot])))
-
-    def descend(slot):
-        downward[slot] = pack_partial(cached(slot))
-
-    def descend_merged(slot):
-        own = cached(slot)
-        send_down(slot).wait_recv()
-        downward[slot] = pack_partial(merge(own, unpack_partial(downward[slot])))
+    save(
+        2,
+        1,
+        both_requests(
+            *[
+                request_partial(
+                    qbuf[me, :, pl.ds(j * SLOT, SLOT)],
+                    own_k[pl.ds(j * SLOT, SLOT), :],
+                    own_v[:, pl.ds(j * SLOT, SLOT)],
+                    True,
+                )
+                for j in range(R_DEV)
+            ]
+        ),
+    )
+
+    def gather_step(step, carry):
+        below = z - 1 - step
+        above = z + 1 + step
+
+        @pl.when(below >= 0)
+        def _():
+            up_whole(below).wait_recv()
+            pl.when(not_last)(lambda: up_whole(below).start())
+            over_late(below).start()
+
+        @pl.when(above < nz)
+        def _():
+            down_whole(above).wait_recv()
+            pl.when(not_first)(lambda: down_whole(above).start())
+            over_late(above).start()
+
+        @pl.when(below >= 0)
+        def _():
+            up_early(below).wait_recv()
+            pl.when(not_last)(lambda: up_early(below).start())
+
+        @pl.when(above < nz)
+        def _():
+            down_early(above).wait_recv()
+            pl.when(not_first)(lambda: down_early(above).start())
+
+        @pl.when(step == 0)
+        def _():
+            loads[1].wait()
+            loads[2].wait()
+
+            def turn(index, inner):
+                cache_vt[index] = vbuf[index].astype(F32).T.astype(BF16)
+                return inner
+
+            lax.fori_loop(0, vbuf.shape[0], turn, 0)
+
+        pl.when(step == min(1, nz - 2))(lambda: save(2, 1, merge(load(2, 1), cached(me))))
+        pl.when(step == min(2, nz - 2))(lambda: save(2, 0, cached(mate)))
+        return carry
+
+    lax.fori_loop(0, nz - 1, gather_step, 0)
+
+    def late_step(plane, carry):
+        @pl.when(plane != z)
+        def _():
+            remote(late(plane, 1 - x), late(plane, 1 - x), qsend.at[4, plane], qrecv.at[2, plane], req=mate).wait_recv()
+
+        return carry
+
+    lax.fori_loop(0, nz, late_step, 0)
+    def send_over(plane):
+        return remote(over.at[0, plane], over.at[1, plane], osend.at[plane], orecv.at[plane], req=mate)
+
+    def send_half(way, plane):
+        there = me + 2 - 4 * way
+        return remote(
+            half_way.at[way, plane], half_way.at[way, plane], psend.at[0, way, plane], precv.at[0, way, plane], req=there
+        )
+
+    def send_full(way, plane):
+        there = me + 2 - 4 * way
+        return remote(
+            full_way.at[way, plane], full_way.at[way, plane], psend.at[1, way, plane], precv.at[1, way, plane], req=there
+        )
+
+    def compute(way, plane):
+        far = cached(plane * 2 + 1 - x)
+        save(way, 0, far)
+        over[0, plane] = pack_partial(far[2:])
+        send_over(plane).start()
+        save(way, 1, cached(plane * 2 + x))
+
+    def finish(way, plane, has_source):
+        @pl.when(has_source)
+        def _():
+            send_half(way, plane).wait_recv()
+            half_way[way, plane] = pack_partial(merge(load(way, 0)[:2], unpack_partial(half_way[way, plane])))
+
+        @pl.when(jnp.logical_not(has_source))
+        def _():
+            half_way[way, plane] = pack_partial(load(way, 0)[:2])
+
+        send_half(way, plane).start()
+        send_over(plane).wait_recv()
+        near = load(way, 1)
+        near = near[:2] + merge(near[2:], unpack_partial(over[1, plane]))
+
+        @pl.when(has_source)
+        def _():
+            send_full(way, plane).wait_recv()
+            full_way[way, plane] = pack_partial(merge(near, unpack_partial(full_way[way, plane])))
+
+        @pl.when(jnp.logical_not(has_source))
+        def _():
+            full_way[way, plane] = pack_partial(near)
+
+        send_full(way, plane).start()
 
     def return_step(step, carry):
-        high = (nz - 1 - step // 2) * 2 + step % 2
+        high = nz - 1 - step
         low = step
-
-        @pl.when(high // 2 > z)
-        def _():
-            pl.when(not_first)(lambda: climb_merged(high))
-            pl.when(z == 0)(lambda: climb(high))
-            send_up(high).start()
-
-        @pl.when(low // 2 < z)
-        def _():
-            pl.when(not_last)(lambda: descend_merged(low))
-            pl.when(z == nz - 1)(lambda: descend(low))
-            send_down(low).start()
-
+        pl.when(high > z)(lambda: compute(0, high))
+        pl.when(low < z)(lambda: compute(1, low))
+        pl.when(high > z)(lambda: finish(0, high, not_first))
+        pl.when(low < z)(lambda: finish(1, low, not_last))
         return carry
 
-    lax.fori_loop(0, (nz - 1) * 2, return_step, 0)
-
-    own = both_requests(
-        *[
-            request_partial(
-                qbuf[me, :, pl.ds(j * SLOT, SLOT)],
-                own_k[pl.ds(j * SLOT, SLOT), :],
-                own_v[:, pl.ds(j * SLOT, SLOT)],
-                True,
-            )
-            for j in range(R_DEV)
-        ]
-    )
-    mine = merge(own, cached(me))
-
-    cross[0] = pack_partial(cached(mate))
-
-    @pl.when(not_first)
-    def _():
-        send_up(mate).wait_recv()
-        cross[0] = pack_partial(merge(unpack_partial(cross[0]), unpack_partial(upward[mate])))
-
-    @pl.when(not_last)
-    def _():
-        send_down(mate).wait_recv()
-        cross[0] = pack_partial(merge(unpack_partial(cross[0]), unpack_partial(downward[mate])))
-
+    over[0, z] = pack_partial(load(2, 0)[2:])
+    send_over(z).start()
+    lax.fori_loop(0, nz - 1, return_step, 0)
+
+    def gather_in(way, condition, send, place, held):
+        @pl.when(condition)
+        def _():
+            send(way, z).wait_recv()
+
+        @pl.when(jnp.logical_not(condition))
+        def _():
+            place[way, z] = jnp.zeros(place.shape[2:], BF16)
+
+        arrived = unpack_partial(place[way, z])
+        arrived = [(numer, jnp.where(condition, top, NEGATIVE), total) for numer, top, total in arrived]
+        return merge(held, arrived)
+
+    half = load(2, 0)[:2]
+    half = gather_in(0, not_first, send_half, half_way, half)
+    half = gather_in(1, not_last, send_half, half_way, half)
+    cross[0] = pack_partial(half)
     to_mate = remote(cross.at[0], cross.at[1], xsend, xrecv, req=mate)
     to_mate.start()
 
@@ -373,34 +434,15 @@
     wo_far = remote(wo_all.at[y_mate], wo_all.at[y_mate], tsend.at[2], trecv.at[2], tp=core_mate)
     wo_far.start()
 
-    nothing = [(jnp.zeros((HDIM, ROWS), F32), jnp.full((1, ROWS), NEGATIVE, F32), jnp.zeros((1, ROWS), F32))] * LOCAL_HEADS
-
-    @pl.when(z == 0)
-    def _():
-        upward[me] = jnp.zeros(upward.shape[1:], BF16)
-
-    @pl.when(not_first)
-    def _():
-        send_up(me).wait_recv()
-
-    @pl.when(z == nz - 1)
-    def _():
-        downward[me] = jnp.zeros(downward.shape[1:], BF16)
-
-    @pl.when(not_last)
-    def _():
-        send_down(me).wait_recv()
-
-    def present(condition, partial):
-        return [
-            (numer, jnp.where(condition, top, empty), total)
-            for (numer, top, total), (_, empty, _) in zip(partial, nothing)
-        ]
-
-    mine = merge(mine, present(not_first, unpack_partial(upward[me])))
-    mine = merge(mine, present(not_last, unpack_partial(downward[me])))
+    loads[3].wait()
+    down_t[...] = down_v[...].astype(F32).T.astype(BF16)
+    send_over(z).wait_recv()
+    mine = load(2, 1)
+    mine = mine[:2] + merge(mine[2:], unpack_partial(over[1, z]))
+    mine = gather_in(0, not_first, send_full, full_way, mine)
+    mine = gather_in(1, not_last, send_full, full_way, mine)
     to_mate.wait_recv()
-    mine = merge(mine, unpack_partial(cross[1]))
+    mine = merge(mine[:2], unpack_partial(cross[1])) + mine[2:]
     att[tp] = jnp.concatenate([(numer / total).astype(BF16) for numer, _, total in mine], axis=0)
 
     att_y = remote(att.at[tp], att.at[tp], tsend.at[3], trecv.at[3], tp=y_mate)
@@ -425,10 +467,10 @@
     terms = terms + projected(diagonal)
 
     middle = (tokens[...].astype(F32) + terms).astype(BF16).astype(F32)
-    normed_middle = normalize(middle, gain_f[...].astype(F32))
+    normed_middle = normalize(middle, gain_f[...].astype(F32)[None, :])
     loads[4].wait()
-    gate = matmul(normed_middle, up_v[...])
-    hidden_t = (gate / (1.0 + jnp.exp(-gate))).T.astype(BF16)
+    gate = matmul_rows(up_v[...], normed_middle)
+    hidden_t = (gate / (1.0 + jnp.exp(-gate))).astype(BF16)
 
     def down_part(index):
         return matmul(down_t[pl.ds(pl.multiple_of(index * WIDTH, 16), WIDTH)], hidden_t)
@@ -450,7 +492,7 @@
     live = jnp.where(lane < SLOT, length[me * R_DEV], length[me * R_DEV + 1])
     swap.wait_recv()
     layer = near_part + y_in[...].astype(F32)
-    out[...] = jnp.where(lane % SLOT < live, layer, 0.0).T.astype(BF16)
+    out[...] = jnp.where(lane % SLOT < live, layer, 0.0).astype(BF16)
 
     over_whole.wait_send()
 
@@ -467,10 +509,18 @@
             down_whole(plane).wait_send()
             down_early(plane).wait_send()
 
-        for column in range(2):
-            slot = plane * 2 + column
-            pl.when(plane > z)(lambda: send_up(slot).wait_send())
-            pl.when(plane < z)(lambda: send_down(slot).wait_send())
+        send_over(plane).wait_send()
+
+        @pl.when(plane > z)
+        def _():
+            send_half(0, plane).wait_send()
+            send_full(0, plane).wait_send()
+
+        @pl.when(plane < z)
+        def _():
+            send_half(1, plane).wait_send()
+            send_full(1, plane).wait_send()
+
         return carry
 
     lax.fori_loop(0, nz, sent_step, 0)
@@ -503,7 +553,7 @@
     away = pl.BlockSpec(memory_space=pl.ANY)
     return pl.pallas_call(
         functools.partial(kernel, nz),
-        out_shape=jax.ShapeDtypeStruct((rows, WIDTH), BF16),
+        out_shape=jax.ShapeDtypeStruct((WIDTH, rows), BF16),
         in_specs=[vmem] * 6 + [away] * 5 + [smem] * 2,
         out_specs=vmem,
         scratch_shapes=[
@@ -511,14 +561,18 @@
             pltpu.VMEM((prefixes, PG, WIDTH), BF16),
             pltpu.VMEM((prefixes, PG, WIDTH), BF16),
             pltpu.VMEM((4, WIDTH, model), BF16),
-            pltpu.VMEM((model, WIDTH), BF16),
+            pltpu.VMEM((WIDTH, model), BF16),
             pltpu.VMEM((WIDTH, model), BF16),
             pltpu.VMEM((model, WIDTH), BF16),
             pltpu.VMEM((ROWS, WIDTH), BF16),
             pltpu.VMEM((WIDTH, ROWS), BF16),
-            pltpu.VMEM((owners, WIDTH + STATS, ROWS), BF16),
-            pltpu.VMEM((owners, WIDTH + STATS, ROWS), BF16),
-            pltpu.VMEM((2, WIDTH + STATS, ROWS), BF16),
+            pltpu.VMEM((prefixes, WIDTH, PG), BF16),
+            pltpu.VMEM((3, 2, WIDTH, ROWS), F32),
+            pltpu.VMEM((3, 2, 2 * LOCAL_HEADS, ROWS), F32),
+            pltpu.VMEM((2, nz, WIDTH + STATS, ROWS), BF16),
+            pltpu.VMEM((2, nz, HALF + STATS, ROWS), BF16),
+            pltpu.VMEM((2, nz, HALF + STATS, ROWS), BF16),
+            pltpu.VMEM((2, HALF + STATS, ROWS), BF16),
             pltpu.VMEM((4, WIDTH, ROWS), BF16),
             pltpu.VMEM((2, WIDTH, ROWS), BF16),
             pltpu.VMEM((2, WIDTH, ROWS), BF16),
@@ -528,31 +582,33 @@
             dma((5,)),
             dma((5, nz)),
             dma((3, nz)),
-            dma((2, owners)),
-            dma((2, owners)),
+            dma((2, 2, nz)),
+            dma((2, 2, nz)),
             dma,
             dma,
             dma((8,)),
             dma((8,)),
+            dma((nz,)),
+            dma((nz,)),
         ],
         compiler_params=pltpu.CompilerParams(
             collective_id=0, has_side_effects=True, vmem_limit_bytes=60 * 1024 * 1024
         ),
     )(
         tokens,
-        attention_gain.reshape(1, model),
-        feedforward_gain.reshape(1, model),
-        query_weight,
-        key_weight,
-        value_weight,
+        attention_gain,
+        feedforward_gain,
+        query_weight.T,
+        key_weight.T,
+        value_weight.T,
         out_weight,
-        up_weight,
+        up_weight.T,
         down_weight,
         cache_keys[0],
         cache_values[0],
         request_prefix,
         suffix_length,
-    )
+    ).T
 
 
 def solution(mesh):

time: 90.7 us -> 73.6 us (0.81)
  the two profiles are of different devices: /device:TPU:18 before, /device:TPU:8 now
where the time goes in v2:
time: 73.6 us; the launch traced here: 73.5 us
  Pallas kernels  71.9 us (98%)
  local copies, waits for them, and re-layouts  1.59 us (2%)
    pallas_call x1, Pallas kernels, per_device(): pl.pallas_call(functools.partial(kernel, nz), out_shape=jax.ShapeDtypeStr...  71.9 us
    unnamed x1, local copies, waits for them, and re-layouts  1.59 us

profile of v2, /device:TPU:8, one launch (start us, length us, event | category | flops | bytes accessed | tf_op | source)
XLA Modules:
  0.0 73.5 jit_solution(11552940453418148934)
XLA Ops:
  0.0 71.9 %shard_map.127 = bf16[320,256]{1,0:T(8,128)(2,1)} custom-call(bf16[256,1280]{1,0:T(8,128)(2,1)} %tokens.1, bf16[1280]{0:T(1024)(128)(2,1)} %gain_a.1, bf16[1280]{0:T(1024)(128)(2,1)} %gain_f.1, bf16[320,1280]{1,0:T(8,128)(2,1)} %bitcast.9, bf16[320,1280]{1,0:T(8,128)(2,1)} %bitcast.10, bf16[320,1280]{1,0:T(8,128)(2,1)} %bitcast.11, bf16[320,1280]{1,0:T(8,128)(2,1)} %wo.1, ...), custom_call_target="tpu_custom_call" | custom-call | tf_op jit(solution)/shard_map/pallas_call | solution.py:554
  71.9 1.6 %copy.15 = bf16[256,320]{0,1:T(8,128)(2,1)} copy(bf16[256,320]{0,1:T(8,128)(2,1)} %bitcast.13) | data formatting | bytes 327680

commit v3 on v2

--- a/solution.py
+++ b/solution.py
@@ -16,7 +16,8 @@
 WIDTH = HDIM * LOCAL_HEADS
 ROWS = R_DEV * SLOT
 STATS = 16
-HALF = WIDTH // 2
+FIRST = HDIM
+REST = WIDTH - HDIM
 
 EPSILON = 1e-06
 NEGATIVE = -1e30
@@ -142,8 +143,8 @@
     cache_vt,
     numers,
     stats,
-    full_way,
-    half_way,
+    rest_way,
+    first_way,
     over,
     cross,
     att,
@@ -213,10 +214,10 @@
         return qbuf.at[plane * 2 + column]
 
     def early(plane, column):
-        return qbuf.at[plane * 2 + column, pl.ds(0, HALF)]
+        return qbuf.at[plane * 2 + column, pl.ds(0, FIRST)]
 
     def late(plane, column):
-        return qbuf.at[plane * 2 + column, pl.ds(HALF, HALF)]
+        return qbuf.at[plane * 2 + column, pl.ds(FIRST, REST)]
 
     def up_whole(plane):
         return remote(whole(plane, x), whole(plane, x), qsend.at[0, plane], qrecv.at[0, plane], req=me + 2)
@@ -253,21 +254,21 @@
     own_k[...] = matmul_rows(normed, wk[...]).astype(BF16)
     own_v[...] = matmul_rows(wv[...], normed).astype(BF16)
 
-    def save(way, column, partial):
-        for h, (numer, top, total) in enumerate(partial):
-            numers[way, column, pl.ds(h * HDIM, HDIM)] = numer
-            stats[way, column, pl.ds(h, 1)] = top
-            stats[way, column, pl.ds(LOCAL_HEADS + h, 1)] = total
-
-    def load(way, column):
-        held = stats[way, column]
+    def save(plane, start, partial):
+        for place, (numer, top, total) in enumerate(partial, start):
+            numers[plane, pl.ds(place * HDIM, HDIM)] = numer
+            stats[plane, pl.ds(place, 1)] = top
+            stats[plane, pl.ds(8 + place, 1)] = total
+
+    def load(plane, start, stop):
+        held = stats[plane]
         return [
             (
-                numers[way, column, pl.ds(h * HDIM, HDIM)],
-                held[h : h + 1],
-                held[LOCAL_HEADS + h : LOCAL_HEADS + h + 1],
+                numers[plane, pl.ds(place * HDIM, HDIM)],
+                held[place : place + 1],
+                held[8 + place : 9 + place],
             )
-            for h in range(LOCAL_HEADS)
+            for place in range(start, stop)
         ]
 
     def cached(target):
@@ -283,7 +284,7 @@
         return both_requests(*parts)
 
     save(
-        2,
+        z,
         1,
         both_requests(
             *[
@@ -298,7 +299,7 @@
         ),
     )
 
-    def gather_step(step, carry):
+    def relay(step):
         below = z - 1 - step
         above = z + 1 + step
 
@@ -324,109 +325,101 @@
             down_early(above).wait_recv()
             pl.when(not_first)(lambda: down_early(above).start())
 
-        @pl.when(step == 0)
-        def _():
-            loads[1].wait()
-            loads[2].wait()
-
-            def turn(index, inner):
-                cache_vt[index] = vbuf[index].astype(F32).T.astype(BF16)
-                return inner
-
-            lax.fori_loop(0, vbuf.shape[0], turn, 0)
-
-        pl.when(step == min(1, nz - 2))(lambda: save(2, 1, merge(load(2, 1), cached(me))))
-        pl.when(step == min(2, nz - 2))(lambda: save(2, 0, cached(mate)))
+    def turn(index, carry):
+        cache_vt[index] = vbuf[index].T
         return carry
 
-    lax.fori_loop(0, nz - 1, gather_step, 0)
-
-    def late_step(plane, carry):
-        @pl.when(plane != z)
-        def _():
-            remote(late(plane, 1 - x), late(plane, 1 - x), qsend.at[4, plane], qrecv.at[2, plane], req=mate).wait_recv()
-
-        return carry
-
-    lax.fori_loop(0, nz, late_step, 0)
+    relay(0)
+    loads[1].wait()
+    loads[2].wait()
+    lax.fori_loop(0, vbuf.shape[0], turn, 0)
+
     def send_over(plane):
         return remote(over.at[0, plane], over.at[1, plane], osend.at[plane], orecv.at[plane], req=mate)
 
-    def send_half(way, plane):
+    def passing(buffer, kind, way, plane):
         there = me + 2 - 4 * way
+        here_slot = jnp.where(jnp.logical_and(way == 1, plane == z), nz, plane)
+        there_slot = jnp.where(jnp.logical_and(way == 1, plane == z - 1), nz, plane)
         return remote(
-            half_way.at[way, plane], half_way.at[way, plane], psend.at[0, way, plane], precv.at[0, way, plane], req=there
+            buffer.at[here_slot],
+            buffer.at[there_slot],
+            psend.at[kind, here_slot],
+            precv.at[kind, there_slot],
+            req=there,
         )
 
-    def send_full(way, plane):
-        there = me + 2 - 4 * way
-        return remote(
-            full_way.at[way, plane], full_way.at[way, plane], psend.at[1, way, plane], precv.at[1, way, plane], req=there
+    def arriving(buffer, kind, way, plane):
+        slot = jnp.where(jnp.logical_and(way == 1, plane == z), nz, plane)
+        copy = remote(
+            buffer.at[slot], buffer.at[slot], psend.at[kind, slot], precv.at[kind, slot], req=me - 2 + 4 * way
         )
-
-    def compute(way, plane):
+        return copy, slot
+
+    def compute(plane):
+        remote(late(plane, 1 - x), late(plane, 1 - x), qsend.at[4, plane], qrecv.at[2, plane], req=mate).wait_recv()
         far = cached(plane * 2 + 1 - x)
-        save(way, 0, far)
-        over[0, plane] = pack_partial(far[2:])
+        save(plane, 0, far[:1])
+        over[0, plane] = pack_partial(far[1:])
         send_over(plane).start()
-        save(way, 1, cached(plane * 2 + x))
+        save(plane, 1, cached(plane * 2 + x))
 
     def finish(way, plane, has_source):
-        @pl.when(has_source)
-        def _():
-            send_half(way, plane).wait_recv()
-            half_way[way, plane] = pack_partial(merge(load(way, 0)[:2], unpack_partial(half_way[way, plane])))
-
-        @pl.when(jnp.logical_not(has_source))
-        def _():
-            half_way[way, plane] = pack_partial(load(way, 0)[:2])
-
-        send_half(way, plane).start()
+        def pass_on(buffer, kind, partial):
+            if has_source:
+                copy, slot = arriving(buffer, kind, way, plane)
+                copy.wait_recv()
+                partial = merge(partial, unpack_partial(buffer[slot]))
+            buffer[plane] = pack_partial(partial)
+            passing(buffer, kind, way, plane).start()
+
+        pass_on(first_way, 0, load(plane, 0, 2))
         send_over(plane).wait_recv()
-        near = load(way, 1)
-        near = near[:2] + merge(near[2:], unpack_partial(over[1, plane]))
-
-        @pl.when(has_source)
-        def _():
-            send_full(way, plane).wait_recv()
-            full_way[way, plane] = pack_partial(merge(near, unpack_partial(full_way[way, plane])))
-
-        @pl.when(jnp.logical_not(has_source))
-        def _():
-            full_way[way, plane] = pack_partial(near)
-
-        send_full(way, plane).start()
+        pass_on(rest_way, 1, merge(load(plane, 2, 5), unpack_partial(over[1, plane])))
 
     def return_step(step, carry):
-        high = nz - 1 - step
-        low = step
-        pl.when(high > z)(lambda: compute(0, high))
-        pl.when(low < z)(lambda: compute(1, low))
-        pl.when(high > z)(lambda: finish(0, high, not_first))
-        pl.when(low < z)(lambda: finish(1, low, not_last))
+        high = z + 1 + step
+        low = z - 1 - step
+        pl.when(high < nz)(lambda: compute(high))
+        pl.when(jnp.logical_and(high < nz, z == 0))(lambda: finish(0, high, False))
+        relay(step + 1)
+        pl.when(low >= 0)(lambda: compute(low))
+        pl.when(jnp.logical_and(low >= 0, z == nz - 1))(lambda: finish(1, low, False))
         return carry
 
-    over[0, z] = pack_partial(load(2, 0)[2:])
+    lax.fori_loop(0, nz - 1, return_step, 0)
+    far = cached(mate)
+    save(z, 0, far[:1])
+    over[0, z] = pack_partial(far[1:])
     send_over(z).start()
-    lax.fori_loop(0, nz - 1, return_step, 0)
-
-    def gather_in(way, condition, send, place, held):
-        @pl.when(condition)
-        def _():
-            send(way, z).wait_recv()
+    save(z, 1, merge(load(z, 1, 5), cached(me)))
+
+    def merge_step(step, carry):
+        distance = nz - 2 - step
+        high = z + distance
+        low = z - distance
+        pl.when(jnp.logical_and(high < nz, not_first))(lambda: finish(0, high, True))
+        pl.when(jnp.logical_and(low >= 0, not_last))(lambda: finish(1, low, True))
+        return carry
+
+    lax.fori_loop(0, nz - 2, merge_step, 0)
+
+    def gather_in(buffer, kind, way, condition, held):
+        copy, slot = arriving(buffer, kind, way, z)
+        pl.when(condition)(lambda: copy.wait_recv())
 
         @pl.when(jnp.logical_not(condition))
         def _():
-            place[way, z] = jnp.zeros(place.shape[2:], BF16)
-
-        arrived = unpack_partial(place[way, z])
+            buffer[slot] = jnp.zeros(buffer.shape[1:], BF16)
+
+        arrived = unpack_partial(buffer[slot])
         arrived = [(numer, jnp.where(condition, top, NEGATIVE), total) for numer, top, total in arrived]
         return merge(held, arrived)
 
-    half = load(2, 0)[:2]
-    half = gather_in(0, not_first, send_half, half_way, half)
-    half = gather_in(1, not_last, send_half, half_way, half)
-    cross[0] = pack_partial(half)
+    firsts = load(z, 0, 2)
+    firsts = gather_in(first_way, 0, 0, not_first, firsts)
+    firsts = gather_in(first_way, 0, 1, not_last, firsts)
+    cross[0] = pack_partial(firsts[:1])
     to_mate = remote(cross.at[0], cross.at[1], xsend, xrecv, req=mate)
     to_mate.start()
 
@@ -435,14 +428,13 @@
     wo_far.start()
 
     loads[3].wait()
-    down_t[...] = down_v[...].astype(F32).T.astype(BF16)
+    down_t[...] = down_v[...].T
     send_over(z).wait_recv()
-    mine = load(2, 1)
-    mine = mine[:2] + merge(mine[2:], unpack_partial(over[1, z]))
-    mine = gather_in(0, not_first, send_full, full_way, mine)
-    mine = gather_in(1, not_last, send_full, full_way, mine)
+    rest = merge(load(z, 2, 5), unpack_partial(over[1, z]))
+    rest = gather_in(rest_way, 1, 0, not_first, rest)
+    rest = gather_in(rest_way, 1, 1, not_last, rest)
     to_mate.wait_recv()
-    mine = merge(mine[:2], unpack_partial(cross[1])) + mine[2:]
+    mine = merge(firsts[1:], unpack_partial(cross[1])) + rest
     att[tp] = jnp.concatenate([(numer / total).astype(BF16) for numer, _, total in mine], axis=0)
 
     att_y = remote(att.at[tp], att.at[tp], tsend.at[3], trecv.at[3], tp=y_mate)
@@ -451,7 +443,7 @@
     att_core.start()
 
     def projected(index):
-        return matmul(att[index].astype(F32).T.astype(BF16), wo_all[index])
+        return matmul(att[index].T, wo_all[index])
 
     terms = projected(tp)
     remote(wo_all.at[core_mate], wo_all.at[core_mate], tsend.at[1], trecv.at[1], tp=core_mate).wait_recv()
@@ -511,15 +503,9 @@
 
         send_over(plane).wait_send()
 
-        @pl.when(plane > z)
-        def _():
-            send_half(0, plane).wait_send()
-            send_full(0, plane).wait_send()
-
-        @pl.when(plane < z)
-        def _():
-            send_half(1, plane).wait_send()
-            send_full(1, plane).wait_send()
+        for kind, buffer in ((0, first_way), (1, rest_way)):
+            pl.when(plane > z)(lambda: passing(buffer, kind, 0, plane).wait_send())
+            pl.when(plane < z)(lambda: passing(buffer, kind, 1, plane).wait_send())
 
         return carry
 
@@ -567,12 +553,12 @@
             pltpu.VMEM((ROWS, WIDTH), BF16),
             pltpu.VMEM((WIDTH, ROWS), BF16),
             pltpu.VMEM((prefixes, WIDTH, PG), BF16),
-            pltpu.VMEM((3, 2, WIDTH, ROWS), F32),
-            pltpu.VMEM((3, 2, 2 * LOCAL_HEADS, ROWS), F32),
-            pltpu.VMEM((2, nz, WIDTH + STATS, ROWS), BF16),
-            pltpu.VMEM((2, nz, HALF + STATS, ROWS), BF16),
-            pltpu.VMEM((2, nz, HALF + STATS, ROWS), BF16),
-            pltpu.VMEM((2, HALF + STATS, ROWS), BF16),
+            pltpu.VMEM((nz, FIRST + WIDTH, ROWS), F32),
+            pltpu.VMEM((nz, STATS, ROWS), F32),
+            pltpu.VMEM((nz + 1, REST + STATS, ROWS), BF16),
+            pltpu.VMEM((nz + 1, 2 * FIRST + STATS, ROWS), BF16),
+            pltpu.VMEM((2, nz, REST + STATS, ROWS), BF16),
+            pltpu.VMEM((2, FIRST + STATS, ROWS), BF16),
             pltpu.VMEM((4, WIDTH, ROWS), BF16),
             pltpu.VMEM((2, WIDTH, ROWS), BF16),
             pltpu.VMEM((2, WIDTH, ROWS), BF16),
@@ -582,8 +568,8 @@
             dma((5,)),
             dma((5, nz)),
             dma((3, nz)),
-            dma((2, 2, nz)),
-            dma((2, 2, nz)),
+            dma((2, nz + 1)),
+            dma((2, nz + 1)),
             dma,
             dma,
             dma((8,)),

time: 73.6 us -> 71.9 us (0.977)
  Pallas kernels: 71.9 us -> 70.1 us
    pallas_call x1, Pallas kernels: 71.9 us -> 70.1 us  [per_device(): pl.pallas_call(functools.partial(kernel, nz), out_shape=jax.ShapeDtypeStr...]
where the time goes in v3:
time: 71.9 us; the launch traced here: 71.7 us
  Pallas kernels  70.1 us (97%)
  local copies, waits for them, and re-layouts  1.59 us (2%)
    pallas_call x1, Pallas kernels, per_device(): pl.pallas_call(functools.partial(kernel, nz), out_shape=jax.ShapeDtypeStr...  70.1 us
    unnamed x1, local copies, waits for them, and re-layouts  1.59 us

profile of v3, /device:TPU:8, one launch (start us, length us, event | category | flops | bytes accessed | tf_op | source)
XLA Modules:
  0.0 71.7 jit_solution(13332569310363318726)
XLA Ops:
  0.0 70.1 %shard_map.127 = bf16[320,256]{1,0:T(8,128)(2,1)} custom-call(bf16[256,1280]{1,0:T(8,128)(2,1)} %tokens.1, bf16[1280]{0:T(1024)(128)(2,1)} %gain_a.1, bf16[1280]{0:T(1024)(128)(2,1)} %gain_f.1, bf16[320,1280]{1,0:T(8,128)(2,1)} %bitcast.9, bf16[320,1280]{1,0:T(8,128)(2,1)} %bitcast.10, bf16[320,1280]{1,0:T(8,128)(2,1)} %bitcast.11, bf16[320,1280]{1,0:T(8,128)(2,1)} %wo.1, ...), custom_call_target="tpu_custom_call" | custom-call | tf_op jit(solution)/shard_map/pallas_call | solution.py:540
  70.1 1.6 %copy.15 = bf16[256,320]{0,1:T(8,128)(2,1)} copy(bf16[256,320]{0,1:T(8,128)(2,1)} %bitcast.13) | data formatting | bytes 327680

commit v4 on v3

--- a/solution.py
+++ b/solution.py
@@ -45,28 +45,30 @@
 
 def request_partial(query_t, keys, values_t, causal):
     none = jnp.zeros((HDIM, SLOT), BF16)
-    spread = jnp.concatenate(
-        [
-            jnp.concatenate(
-                [head_rows(query_t, h) if g == h else none for g in range(LOCAL_HEADS)], axis=1
-            )
-            for h in range(LOCAL_HEADS)
-        ],
-        axis=0,
-    )
-    scores = matmul(keys, spread) * (1.0 / math.sqrt(HDIM))
-    if causal:
-        key_row = lax.broadcasted_iota(jnp.int32, scores.shape, 0)
-        query_row = lax.broadcasted_iota(jnp.int32, scores.shape, 1) % SLOT
-        scores = jnp.where(key_row <= query_row, scores, NEGATIVE)
-    top = jnp.max(scores, axis=0, keepdims=True)
-    if not causal:
-        top = top.astype(BF16).astype(F32)
-    weights = jnp.exp(scores - top)
-    total = jnp.sum(weights, axis=0, keepdims=True)
-    numer = matmul(values_t, weights.astype(BF16))
-    lanes = [slice(h * SLOT, (h + 1) * SLOT) for h in range(LOCAL_HEADS)]
-    return [(head_rows(numer, h)[:, lanes[h]], top[:, lanes[h]], total[:, lanes[h]]) for h in range(LOCAL_HEADS)]
+    partial = []
+    for pair, (start, stop) in enumerate(((0, 256), (128, WIDTH))):
+        first, second = head_rows(query_t, 2 * pair), head_rows(query_t, 2 * pair + 1)
+        above = 2 * pair * HDIM - start
+        below = stop - start - above - 2 * HDIM
+        blocks = [jnp.zeros((above, 2 * SLOT), BF16)] if above else []
+        blocks.append(jnp.concatenate([first, none], axis=1))
+        blocks.append(jnp.concatenate([none, second], axis=1))
+        if below:
+            blocks.append(jnp.zeros((below, 2 * SLOT), BF16))
+        scores = matmul(keys[:, start:stop], jnp.concatenate(blocks, axis=0)) * (1.0 / math.sqrt(HDIM))
+        if causal:
+            key_row = lax.broadcasted_iota(jnp.int32, scores.shape, 0)
+            query_row = lax.broadcasted_iota(jnp.int32, scores.shape, 1) % SLOT
+            scores = jnp.where(key_row <= query_row, scores, NEGATIVE)
+        top = jnp.max(scores, axis=0, keepdims=True)
+        if not causal:
+            top = top.astype(BF16).astype(F32)
+        weights = jnp.exp(scores - top)
+        total = jnp.sum(weights, axis=0, keepdims=True)
+        numer = matmul(values_t[2 * pair * HDIM : 2 * (pair + 1) * HDIM], weights.astype(BF16))
+        partial.append((numer[:HDIM, :SLOT], top[:, :SLOT], total[:, :SLOT]))
+        partial.append((numer[HDIM:, SLOT:], top[:, SLOT:], total[:, SLOT:]))
+    return partial
 
 
 def both_requests(first, second):
@@ -164,6 +166,8 @@
     trecv,
     osend,
     orecv,
+    wk_v,
+    wv_v,
 ):
     me = lax.axis_index("req")
     tp = lax.axis_index("tp")
@@ -199,7 +203,7 @@
     loads = [
         pltpu.make_async_copy(source, target, local_sem.at[i])
         for i, (source, target) in enumerate(
-            [(wo, wo_all.at[tp]), (cache_k, kbuf), (cache_v, vbuf), (wdown, down_v), (wup, up_v)]
+            [(wo, wo_all.at[tp]), (cache_k, kbuf), (cache_v, vbuf), (wdown, down_v), (wup, up_v), (wk, wk_v), (wv, wv_v)]
         )
     ]
     for load in loads:
@@ -251,8 +255,10 @@
     pl.when(not_last)(lambda: up_early(z).start())
     pl.when(not_first)(lambda: down_early(z).start())
 
-    own_k[...] = matmul_rows(normed, wk[...]).astype(BF16)
-    own_v[...] = matmul_rows(wv[...], normed).astype(BF16)
+    loads[5].wait()
+    loads[6].wait()
+    own_k[...] = matmul_rows(normed, wk_v[...]).astype(BF16)
+    own_v[...] = matmul_rows(wv_v[...], normed).astype(BF16)
 
     def save(plane, start, partial):
         for place, (numer, top, total) in enumerate(partial, start):
@@ -388,18 +394,21 @@
         return carry
 
     lax.fori_loop(0, nz - 1, return_step, 0)
-    far = cached(mate)
-    save(z, 0, far[:1])
-    over[0, z] = pack_partial(far[1:])
-    send_over(z).start()
-    save(z, 1, merge(load(z, 1, 5), cached(me)))
-
     def merge_step(step, carry):
         distance = nz - 2 - step
         high = z + distance
         low = z - distance
         pl.when(jnp.logical_and(high < nz, not_first))(lambda: finish(0, high, True))
         pl.when(jnp.logical_and(low >= 0, not_last))(lambda: finish(1, low, True))
+
+        @pl.when(step == 0)
+        def _():
+            far = cached(mate)
+            save(z, 0, far[:1])
+            over[0, z] = pack_partial(far[1:])
+            send_over(z).start()
+            save(z, 1, merge(load(z, 1, 5), cached(me)))
+
         return carry
 
     lax.fori_loop(0, nz - 2, merge_step, 0)
@@ -540,7 +549,7 @@
     return pl.pallas_call(
         functools.partial(kernel, nz),
         out_shape=jax.ShapeDtypeStruct((WIDTH, rows), BF16),
-        in_specs=[vmem] * 6 + [away] * 5 + [smem] * 2,
+        in_specs=[vmem] * 4 + [away] * 7 + [smem] * 2,
         out_specs=vmem,
         scratch_shapes=[
             pltpu.VMEM((owners, WIDTH, ROWS), BF16),
@@ -565,7 +574,7 @@
             pltpu.VMEM((WIDTH, ROWS), BF16),
             pltpu.VMEM((WIDTH, ROWS), BF16),
             pltpu.VMEM((model, ROWS), F32),
-            dma((5,)),
+            dma((7,)),
             dma((5, nz)),
             dma((3, nz)),
             dma((2, nz + 1)),
@@ -576,6 +585,8 @@
             dma((8,)),
             dma((nz,)),
             dma((nz,)),
+            pltpu.VMEM((WIDTH, model), BF16),
+            pltpu.VMEM((WIDTH, model), BF16),
         ],
         compiler_params=pltpu.CompilerParams(
             collective_id=0, has_side_effects=True, vmem_limit_bytes=60 * 1024 * 1024

time: 71.9 us -> 72.9 us (1.014)
  the two profiles are of different devices: /device:TPU:8 before, /device:TPU:0 now
where the time goes in v4:
time: 72.9 us; the launch traced here: 72.7 us
  Pallas kernels  71.1 us (98%)
  local copies, waits for them, and re-layouts  1.59 us (2%)
    pallas_call x1, Pallas kernels, per_device(): pl.pallas_call(functools.partial(kernel, nz), out_shape=jax.ShapeDtypeStr...  71.1 us
    unnamed x1, local copies, waits for them, and re-layouts  1.59 us

profile of v4, /device:TPU:0, one launch (start us, length us, event | category | flops | bytes accessed | tf_op | source)
XLA Modules:
  0.0 72.7 jit_solution(518113763864028185)
XLA Ops:
  0.0 71.1 %shard_map.127 = bf16[320,256]{1,0:T(8,128)(2,1)} custom-call(bf16[256,1280]{1,0:T(8,128)(2,1)} %tokens.1, bf16[1280]{0:T(1024)(128)(2,1)} %gain_a.1, bf16[1280]{0:T(1024)(128)(2,1)} %gain_f.1, bf16[320,1280]{1,0:T(8,128)(2,1)} %bitcast.9, bf16[320,1280]{1,0:T(8,128)(2,1)} %bitcast.10, bf16[320,1280]{1,0:T(8,128)(2,1)} %bitcast.11, bf16[320,1280]{1,0:T(8,128)(2,1)} %wo.1, ...), custom_call_target="tpu_custom_call" | custom-call | tf_op jit(solution)/shard_map/pallas_call | solution.py:549
  71.1 1.6 %copy.15 = bf16[256,320]{0,1:T(8,128)(2,1)} copy(bf16[256,320]{0,1:T(8,128)(2,1)} %bitcast.13) | data formatting | bytes 327680

commit v5 on v4

--- a/solution.py
+++ b/solution.py
@@ -199,6 +199,9 @@
     greet(tp=y_mate)
     pl.when(not_first)(lambda: greet(req=me - 2))
     pl.when(not_last)(lambda: greet(req=me + 2))
+    span = 2 * (nz - 1)
+    pl.when(jnp.logical_not(not_first))(lambda: greet(req=me + span))
+    pl.when(jnp.logical_not(not_last))(lambda: greet(req=me - span))
 
     loads = [
         pltpu.make_async_copy(source, target, local_sem.at[i])
@@ -212,7 +215,7 @@
     normed = normalize(tokens[...].astype(F32), gain_a[...].astype(F32)[None, :])
     qbuf[me] = matmul_rows(wq[...], normed).astype(BF16)
 
-    pl.semaphore_wait(barrier, 3 + jnp.where(not_first, 1, 0) + jnp.where(not_last, 1, 0))
+    pl.semaphore_wait(barrier, 5)
 
     def whole(plane, column):
         return qbuf.at[plane * 2 + column]
@@ -344,23 +347,20 @@
         return remote(over.at[0, plane], over.at[1, plane], osend.at[plane], orecv.at[plane], req=mate)
 
     def passing(buffer, kind, way, plane):
-        there = me + 2 - 4 * way
-        here_slot = jnp.where(jnp.logical_and(way == 1, plane == z), nz, plane)
-        there_slot = jnp.where(jnp.logical_and(way == 1, plane == z - 1), nz, plane)
+        if way == 0:
+            direct = jnp.logical_and(z == 0, plane == nz - 1)
+            there = me + jnp.where(direct, span, 2)
+            there_slot = jnp.where(direct, nz, plane)
+        else:
+            direct = jnp.logical_and(z == nz - 1, plane == 0)
+            there = me - jnp.where(direct, span, 2)
+            there_slot = jnp.where(plane == z - 1, nz, plane)
         return remote(
-            buffer.at[here_slot],
-            buffer.at[there_slot],
-            psend.at[kind, here_slot],
-            precv.at[kind, there_slot],
-            req=there,
+            buffer.at[plane], buffer.at[there_slot], psend.at[kind, plane], precv.at[kind, there_slot], req=there
         )
 
-    def arriving(buffer, kind, way, plane):
-        slot = jnp.where(jnp.logical_and(way == 1, plane == z), nz, plane)
-        copy = remote(
-            buffer.at[slot], buffer.at[slot], psend.at[kind, slot], precv.at[kind, slot], req=me - 2 + 4 * way
-        )
-        return copy, slot
+    def arriving(buffer, kind, slot):
+        return remote(buffer.at[slot], buffer.at[slot], psend.at[kind, slot], precv.at[kind, slot], req=mate)
 
     def compute(plane):
         remote(late(plane, 1 - x), late(plane, 1 - x), qsend.at[4, plane], qrecv.at[2, plane], req=mate).wait_recv()
@@ -373,9 +373,8 @@
     def finish(way, plane, has_source):
         def pass_on(buffer, kind, partial):
             if has_source:
-                copy, slot = arriving(buffer, kind, way, plane)
-                copy.wait_recv()
-                partial = merge(partial, unpack_partial(buffer[slot]))
+                arriving(buffer, kind, plane).wait_recv()
+                partial = merge(partial, unpack_partial(buffer[plane]))
             buffer[plane] = pack_partial(partial)
             passing(buffer, kind, way, plane).start()
 
@@ -386,48 +385,38 @@
     def return_step(step, carry):
         high = z + 1 + step
         low = z - 1 - step
+        starts_up = jnp.logical_or(z == 0, jnp.logical_and(z == 1, high == nz - 1))
+        starts_down = jnp.logical_or(z == nz - 1, jnp.logical_and(z == nz - 2, low == 0))
         pl.when(high < nz)(lambda: compute(high))
-        pl.when(jnp.logical_and(high < nz, z == 0))(lambda: finish(0, high, False))
+        pl.when(jnp.logical_and(high < nz, starts_up))(lambda: finish(0, high, False))
         relay(step + 1)
         pl.when(low >= 0)(lambda: compute(low))
-        pl.when(jnp.logical_and(low >= 0, z == nz - 1))(lambda: finish(1, low, False))
+        pl.when(jnp.logical_and(low >= 0, starts_down))(lambda: finish(1, low, False))
         return carry
 
     lax.fori_loop(0, nz - 1, return_step, 0)
     def merge_step(step, carry):
-        distance = nz - 2 - step
+        distance = nz - 3 - step
         high = z + distance
         low = z - distance
         pl.when(jnp.logical_and(high < nz, not_first))(lambda: finish(0, high, True))
         pl.when(jnp.logical_and(low >= 0, not_last))(lambda: finish(1, low, True))
-
-        @pl.when(step == 0)
-        def _():
-            far = cached(mate)
-            save(z, 0, far[:1])
-            over[0, z] = pack_partial(far[1:])
-            send_over(z).start()
-            save(z, 1, merge(load(z, 1, 5), cached(me)))
-
         return carry
 
-    lax.fori_loop(0, nz - 2, merge_step, 0)
-
-    def gather_in(buffer, kind, way, condition, held):
-        copy, slot = arriving(buffer, kind, way, z)
-        pl.when(condition)(lambda: copy.wait_recv())
-
-        @pl.when(jnp.logical_not(condition))
-        def _():
-            buffer[slot] = jnp.zeros(buffer.shape[1:], BF16)
-
-        arrived = unpack_partial(buffer[slot])
-        arrived = [(numer, jnp.where(condition, top, NEGATIVE), total) for numer, top, total in arrived]
-        return merge(held, arrived)
+    lax.fori_loop(0, nz - 3, merge_step, 0)
+    far = cached(mate)
+    save(z, 0, far[:1])
+    over[0, z] = pack_partial(far[1:])
+    send_over(z).start()
+    save(z, 1, merge(load(z, 1, 5), cached(me)))
+
+    def gather_in(buffer, kind, slot, held):
+        arriving(buffer, kind, slot).wait_recv()
+        return merge(held, unpack_partial(buffer[slot]))
 
     firsts = load(z, 0, 2)
-    firsts = gather_in(first_way, 0, 0, not_first, firsts)
-    firsts = gather_in(first_way, 0, 1, not_last, firsts)
+    firsts = gather_in(first_way, 0, z, firsts)
+    firsts = gather_in(first_way, 0, nz, firsts)
     cross[0] = pack_partial(firsts[:1])
     to_mate = remote(cross.at[0], cross.at[1], xsend, xrecv, req=mate)
     to_mate.start()
@@ -440,8 +429,8 @@
     down_t[...] = down_v[...].T
     send_over(z).wait_recv()
     rest = merge(load(z, 2, 5), unpack_partial(over[1, z]))
-    rest = gather_in(rest_way, 1, 0, not_first, rest)
-    rest = gather_in(rest_way, 1, 1, not_last, rest)
+    rest = gather_in(rest_way, 1, z, rest)
+    rest = gather_in(rest_way, 1, nz, rest)
     to_mate.wait_recv()
     mine = merge(firsts[1:], unpack_partial(cross[1])) + rest
     att[tp] = jnp.concatenate([(numer / total).astype(BF16) for numer, _, total in mine], axis=0)
@@ -477,17 +466,20 @@
         return matmul(down_t[pl.ds(pl.multiple_of(index * WIDTH, 16), WIDTH)], hidden_t)
 
     core_out[0] = down_part(diagonal).astype(BF16)
-    core_out[1] = down_part(core_mate).astype(BF16)
-    fold = remote(core_out, core_in, tsend.at[6], trecv.at[6], tp=core_mate)
+    fold = remote(core_out.at[0], core_in.at[0], tsend.at[6], trecv.at[6], tp=core_mate)
     fold.start()
     far_part = down_part(y_mate)
-    near_part = down_part(tp)
-    mid_t[...] = middle.T
-    near_part = near_part + mid_t[pl.ds(pl.multiple_of(tp * WIDTH, 16), WIDTH)]
+    core_out[1] = down_part(core_mate).astype(BF16)
+    fold_near = remote(core_out.at[1], core_in.at[1], tsend.at[8], trecv.at[8], tp=core_mate)
+    fold_near.start()
     fold.wait_recv()
     y_out[...] = (far_part + core_in[0].astype(F32)).astype(BF16)
     swap = remote(y_out, y_in, tsend.at[7], trecv.at[7], tp=y_mate)
     swap.start()
+    near_part = down_part(tp)
+    mid_t[...] = middle.T
+    near_part = near_part + mid_t[pl.ds(pl.multiple_of(tp * WIDTH, 16), WIDTH)]
+    fold_near.wait_recv()
     near_part = near_part + core_in[1].astype(F32)
     lane = lax.broadcasted_iota(jnp.int32, (WIDTH, ROWS), 1)
     live = jnp.where(lane < SLOT, length[me * R_DEV], length[me * R_DEV + 1])
@@ -519,7 +511,7 @@
         return carry
 
     lax.fori_loop(0, nz, sent_step, 0)
-    for copy in (to_mate, wo_y, wo_core, wo_far, att_y, att_core, att_far, fold, swap):
+    for copy in (to_mate, wo_y, wo_core, wo_far, att_y, att_core, att_far, fold, fold_near, swap):
         copy.wait_send()
 
 
@@ -581,8 +573,8 @@
             dma((2, nz + 1)),
             dma,
             dma,
-            dma((8,)),
-            dma((8,)),
+            dma((9,)),
+            dma((9,)),
             dma((nz,)),
             dma((nz,)),
             pltpu.VMEM((WIDTH, model), BF16),

time: 72.9 us -> 66.5 us (0.912)
  Pallas kernels: 71.1 us -> 64.7 us
    pallas_call x1, Pallas kernels: 71.1 us -> 64.7 us  [per_device(): pl.pallas_call(functools.partial(kernel, nz), out_shape=jax.ShapeDtypeStr...]
where the time goes in v5:
time: 66.5 us; the launch traced here: 66.3 us
  Pallas kernels  64.7 us (97%)
  local copies, waits for them, and re-layouts  1.59 us (2%)
    pallas_call x1, Pallas kernels, per_device(): pl.pallas_call(functools.partial(kernel, nz), out_shape=jax.ShapeDtypeStr...  64.7 us
    unnamed x1, local copies, waits for them, and re-layouts  1.59 us

profile of v5, /device:TPU:0, one launch (start us, length us, event | category | flops | bytes accessed | tf_op | source)
XLA Modules:
  0.0 66.3 jit_solution(1738348839636174634)
XLA Ops:
  0.0 64.7 %shard_map.127 = bf16[320,256]{1,0:T(8,128)(2,1)} custom-call(bf16[256,1280]{1,0:T(8,128)(2,1)} %tokens.1, bf16[1280]{0:T(1024)(128)(2,1)} %gain_a.1, bf16[1280]{0:T(1024)(128)(2,1)} %gain_f.1, bf16[320,1280]{1,0:T(8,128)(2,1)} %bitcast.9, bf16[320,1280]{1,0:T(8,128)(2,1)} %bitcast.10, bf16[320,1280]{1,0:T(8,128)(2,1)} %bitcast.11, bf16[320,1280]{1,0:T(8,128)(2,1)} %wo.1, ...), custom_call_target="tpu_custom_call" | custom-call | tf_op jit(solution)/shard_map/pallas_call | solution.py:541
  64.7 1.6 %copy.15 = bf16[256,320]{0,1:T(8,128)(2,1)} copy(bf16[256,320]{0,1:T(8,128)(2,1)} %bitcast.13) | data formatting | bytes 327680

commit v6 on v5

--- a/solution.py
+++ b/solution.py
@@ -248,20 +248,9 @@
     pl.when(not_last)(lambda: up_whole(z).start())
     pl.when(not_first)(lambda: down_whole(z).start())
 
-    loads[0].wait()
-    wo_y = remote(wo_all.at[tp], wo_all.at[tp], tsend.at[0], trecv.at[0], tp=y_mate)
-    wo_core = remote(wo_all.at[tp], wo_all.at[tp], tsend.at[1], trecv.at[1], tp=core_mate)
-    wo_y.start()
-    wo_core.start()
-
     got_whole.wait_recv()
     pl.when(not_last)(lambda: up_early(z).start())
     pl.when(not_first)(lambda: down_early(z).start())
-
-    loads[5].wait()
-    loads[6].wait()
-    own_k[...] = matmul_rows(normed, wk_v[...]).astype(BF16)
-    own_v[...] = matmul_rows(wv_v[...], normed).astype(BF16)
 
     def save(plane, start, partial):
         for place, (numer, top, total) in enumerate(partial, start):
@@ -292,6 +281,115 @@
             )
         return both_requests(*parts)
 
+    def relay(step):
+        below = z - 1 - step
+        above = z + 1 + step
+
+        @pl.when(below >= 0)
+        def _():
+            up_whole(below).wait_recv()
+            pl.when(not_last)(lambda: up_whole(below).start())
+            over_late(below).start()
+
+        @pl.when(above < nz)
+        def _():
+            down_whole(above).wait_recv()
+            pl.when(not_first)(lambda: down_whole(above).start())
+            over_late(above).start()
+
+        @pl.when(below >= 0)
+        def _():
+            up_early(below).wait_recv()
+            pl.when(not_last)(lambda: up_early(below).start())
+
+        @pl.when(above < nz)
+        def _():
+            down_early(above).wait_recv()
+            pl.when(not_first)(lambda: down_early(above).start())
+
+    def turn(index, carry):
+        cache_vt[index] = vbuf[index].T
+        return carry
+
+    loads[2].wait()
+    lax.fori_loop(0, vbuf.shape[0], turn, 0)
+
+    loads[0].wait()
+    wo_y = remote(wo_all.at[tp], wo_all.at[tp], tsend.at[0], trecv.at[0], tp=y_mate)
+    wo_core = remote(wo_all.at[tp], wo_all.at[tp], tsend.at[1], trecv.at[1], tp=core_mate)
+    wo_y.start()
+    wo_core.start()
+    loads[1].wait()
+    relay(0)
+    def send_over(plane):
+        return remote(over.at[0, plane], over.at[1, plane], osend.at[plane], orecv.at[plane], req=mate)
+
+    def passing(buffer, kind, way, plane):
+        if way == 0:
+            direct = jnp.logical_and(z == 0, plane == nz - 1)
+            there = me + jnp.where(direct, span, 2)
+            there_slot = jnp.where(direct, nz, plane)
+        else:
+            direct = jnp.logical_and(z == nz - 1, plane == 0)
+            there = me - jnp.where(direct, span, 2)
+            there_slot = jnp.where(plane == z - 1, nz, plane)
+        return remote(
+            buffer.at[plane], buffer.at[there_slot], psend.at[kind, plane], precv.at[kind, there_slot], req=there
+        )
+
+    def arriving(buffer, kind, slot):
+        return remote(buffer.at[slot], buffer.at[slot], psend.at[kind, slot], precv.at[kind, slot], req=mate)
+
+    def compute(plane):
+        remote(late(plane, 1 - x), late(plane, 1 - x), qsend.at[4, plane], qrecv.at[2, plane], req=mate).wait_recv()
+        far = cached(plane * 2 + 1 - x)
+        save(plane, 0, far[:1])
+        over[0, plane] = pack_partial(far[1:])
+        send_over(plane).start()
+        save(plane, 1, cached(plane * 2 + x))
+
+    def finish(way, plane, has_source):
+        def pass_on(buffer, kind, partial):
+            if has_source:
+                arriving(buffer, kind, plane).wait_recv()
+                partial = merge(partial, unpack_partial(buffer[plane]))
+            buffer[plane] = pack_partial(partial)
+            passing(buffer, kind, way, plane).start()
+
+        pass_on(first_way, 0, load(plane, 0, 2))
+        send_over(plane).wait_recv()
+        pass_on(rest_way, 1, merge(load(plane, 2, 5), unpack_partial(over[1, plane])))
+
+    def return_step(step, carry):
+        high = z + 1 + step
+        low = z - 1 - step
+        starts_up = jnp.logical_or(z == 0, jnp.logical_and(z == 1, high == nz - 1))
+        starts_down = jnp.logical_or(z == nz - 1, jnp.logical_and(z == nz - 2, low == 0))
+        pl.when(high < nz)(lambda: compute(high))
+        pl.when(jnp.logical_and(high < nz, starts_up))(lambda: finish(0, high, False))
+        relay(step + 1)
+        pl.when(low >= 0)(lambda: compute(low))
+        pl.when(jnp.logical_and(low >= 0, starts_down))(lambda: finish(1, low, False))
+        return carry
+
+    lax.fori_loop(0, nz - 1, return_step, 0)
+    def merge_step(step, carry):
+        distance = nz - 3 - step
+        high = z + distance
+        low = z - distance
+        pl.when(jnp.logical_and(high < nz, not_first))(lambda: finish(0, high, True))
+        pl.when(jnp.logical_and(low >= 0, not_last))(lambda: finish(1, low, True))
+        return carry
+
+    lax.fori_loop(0, nz - 3, merge_step, 0)
+    far = cached(mate)
+    save(z, 0, far[:1])
+    over[0, z] = pack_partial(far[1:])
+    send_over(z).start()
+    loads[5].wait()
+    loads[6].wait()
+    own_k[...] = matmul_rows(normed, wk_v[...]).astype(BF16)
+    own_v[...] = matmul_rows(wv_v[...], normed).astype(BF16)
     save(
         z,
         1,
@@ -307,107 +405,6 @@
             ]
         ),
     )
-
-    def relay(step):
-        below = z - 1 - step
-        above = z + 1 + step
-
-        @pl.when(below >= 0)
-        def _():
-            up_whole(below).wait_recv()
-            pl.when(not_last)(lambda: up_whole(below).start())
-            over_late(below).start()
-
-        @pl.when(above < nz)
-        def _():
-            down_whole(above).wait_recv()
-            pl.when(not_first)(lambda: down_whole(above).start())
-            over_late(above).start()
-
-        @pl.when(below >= 0)
-        def _():
-            up_early(below).wait_recv()
-            pl.when(not_last)(lambda: up_early(below).start())
-
-        @pl.when(above < nz)
-        def _():
-            down_early(above).wait_recv()
-            pl.when(not_first)(lambda: down_early(above).start())
-
-    def turn(index, carry):
-        cache_vt[index] = vbuf[index].T
-        return carry
-
-    relay(0)
-    loads[1].wait()
-    loads[2].wait()
-    lax.fori_loop(0, vbuf.shape[0], turn, 0)
-
-    def send_over(plane):
-        return remote(over.at[0, plane], over.at[1, plane], osend.at[plane], orecv.at[plane], req=mate)
-
-    def passing(buffer, kind, way, plane):
-        if way == 0:
-            direct = jnp.logical_and(z == 0, plane == nz - 1)
-            there = me + jnp.where(direct, span, 2)
-            there_slot = jnp.where(direct, nz, plane)
-        else:
-            direct = jnp.logical_and(z == nz - 1, plane == 0)
-            there = me - jnp.where(direct, span, 2)
-            there_slot = jnp.where(plane == z - 1, nz, plane)
-        return remote(
-            buffer.at[plane], buffer.at[there_slot], psend.at[kind, plane], precv.at[kind, there_slot], req=there
-        )
-
-    def arriving(buffer, kind, slot):
-        return remote(buffer.at[slot], buffer.at[slot], psend.at[kind, slot], precv.at[kind, slot], req=mate)
-
-    def compute(plane):
-        remote(late(plane, 1 - x), late(plane, 1 - x), qsend.at[4, plane], qrecv.at[2, plane], req=mate).wait_recv()
-        far = cached(plane * 2 + 1 - x)
-        save(plane, 0, far[:1])
-        over[0, plane] = pack_partial(far[1:])
-        send_over(plane).start()
-        save(plane, 1, cached(plane * 2 + x))
-
-    def finish(way, plane, has_source):
-        def pass_on(buffer, kind, partial):
-            if has_source:
-                arriving(buffer, kind, plane).wait_recv()
-                partial = merge(partial, unpack_partial(buffer[plane]))
-            buffer[plane] = pack_partial(partial)
-            passing(buffer, kind, way, plane).start()
-
-        pass_on(first_way, 0, load(plane, 0, 2))
-        send_over(plane).wait_recv()
-        pass_on(rest_way, 1, merge(load(plane, 2, 5), unpack_partial(over[1, plane])))
-
-    def return_step(step, carry):
-        high = z + 1 + step
-        low = z - 1 - step
-        starts_up = jnp.logical_or(z == 0, jnp.logical_and(z == 1, high == nz - 1))
-        starts_down = jnp.logical_or(z == nz - 1, jnp.logical_and(z == nz - 2, low == 0))
-        pl.when(high < nz)(lambda: compute(high))
-        pl.when(jnp.logical_and(high < nz, starts_up))(lambda: finish(0, high, False))
-        relay(step + 1)
-        pl.when(low >= 0)(lambda: compute(low))
-        pl.when(jnp.logical_and(low >= 0, starts_down))(lambda: finish(1, low, False))
-        return carry
-
-    lax.fori_loop(0, nz - 1, return_step, 0)
-    def merge_step(step, carry):
-        distance = nz - 3 - step
-        high = z + distance
-        low = z - distance
-        pl.when(jnp.logical_and(high < nz, not_first))(lambda: finish(0, high, True))
-        pl.when(jnp.logical_and(low >= 0, not_last))(lambda: finish(1, low, True))
-        return carry
-
-    lax.fori_loop(0, nz - 3, merge_step, 0)
-    far = cached(mate)
-    save(z, 0, far[:1])
-    over[0, z] = pack_partial(far[1:])
-    send_over(z).start()
     save(z, 1, merge(load(z, 1, 5), cached(me)))
 
     def gather_in(buffer, kind, slot, held):

time: 66.5 us -> 67.5 us (1.015)
  Pallas kernels: 64.7 us -> 65.8 us
    pallas_call x1, Pallas kernels: 64.7 us -> 65.8 us  [per_device(): pl.pallas_call(functools.partial(kernel, nz), out_shape=jax.ShapeDtypeStr...]
where the time goes in v6:
time: 67.5 us; the launch traced here: 67.4 us
  Pallas kernels  65.8 us (97%)
  local copies, waits for them, and re-layouts  1.59 us (2%)
    pallas_call x1, Pallas kernels, per_device(): pl.pallas_call(functools.partial(kernel, nz), out_shape=jax.ShapeDtypeStr...  65.8 us
    unnamed x1, local copies, waits for them, and re-layouts  1.59 us

profile of v6, /device:TPU:0, one launch (start us, length us, event | category | flops | bytes accessed | tf_op | source)
XLA Modules:
  0.0 67.4 jit_solution(1570571974193571599)
XLA Ops:
  0.0 65.8 %shard_map.127 = bf16[320,256]{1,0:T(8,128)(2,1)} custom-call(bf16[256,1280]{1,0:T(8,128)(2,1)} %tokens.1, bf16[1280]{0:T(1024)(128)(2,1)} %gain_a.1, bf16[1280]{0:T(1024)(128)(2,1)} %gain_f.1, bf16[320,1280]{1,0:T(8,128)(2,1)} %bitcast.9, bf16[320,1280]{1,0:T(8,128)(2,1)} %bitcast.10, bf16[320,1280]{1,0:T(8,128)(2,1)} %bitcast.11, bf16[320,1280]{1,0:T(8,128)(2,1)} %wo.1, ...), custom_call_target="tpu_custom_call" | custom-call | tf_op jit(solution)/shard_map/pallas_call | solution.py:538
  65.8 1.6 %copy.15 = bf16[256,320]{0,1:T(8,128)(2,1)} copy(bf16[256,320]{0,1:T(8,128)(2,1)} %bitcast.13) | data formatting | bytes 327680

commit v7 on v5

--- a/solution.py
+++ b/solution.py
@@ -248,12 +248,6 @@
     pl.when(not_last)(lambda: up_whole(z).start())
     pl.when(not_first)(lambda: down_whole(z).start())
 
-    loads[0].wait()
-    wo_y = remote(wo_all.at[tp], wo_all.at[tp], tsend.at[0], trecv.at[0], tp=y_mate)
-    wo_core = remote(wo_all.at[tp], wo_all.at[tp], tsend.at[1], trecv.at[1], tp=core_mate)
-    wo_y.start()
-    wo_core.start()
-
     got_whole.wait_recv()
     pl.when(not_last)(lambda: up_early(z).start())
     pl.when(not_first)(lambda: down_early(z).start())
@@ -394,6 +388,11 @@
         pl.when(jnp.logical_and(low >= 0, starts_down))(lambda: finish(1, low, False))
         return carry
 
+    loads[0].wait()
+    wo_y = remote(wo_all.at[tp], wo_all.at[tp], tsend.at[0], trecv.at[0], tp=y_mate)
+    wo_core = remote(wo_all.at[tp], wo_all.at[tp], tsend.at[1], trecv.at[1], tp=core_mate)
+    wo_y.start()
+    wo_core.start()
     lax.fori_loop(0, nz - 1, return_step, 0)
     def merge_step(step, carry):
         distance = nz - 3 - step

time: 66.5 us -> 66.1 us (level)
  Pallas kernels: 64.7 us -> 63.8 us
    pallas_call x1, Pallas kernels: 64.7 us -> 63.8 us  [per_device(): pl.pallas_call(functools.partial(kernel, nz), out_shape=jax.ShapeDtypeStr...]
where the time goes in v7:
time: 66.1 us; the launch traced here: 65.4 us
  Pallas kernels  63.8 us (97%)
  local copies, waits for them, and re-layouts  1.59 us (2%)
    pallas_call x1, Pallas kernels, per_device(): pl.pallas_call(functools.partial(kernel, nz), out_shape=jax.ShapeDtypeStr...  63.8 us
    unnamed x1, local copies, waits for them, and re-layouts  1.59 us

profile of v7, /device:TPU:0, one launch (start us, length us, event | category | flops | bytes accessed | tf_op | source)
XLA Modules:
  0.0 65.4 jit_solution(10061174326272890741)
XLA Ops:
  0.0 63.8 %shard_map.127 = bf16[320,256]{1,0:T(8,128)(2,1)} custom-call(bf16[256,1280]{1,0:T(8,128)(2,1)} %tokens.1, bf16[1280]{0:T(1024)(128)(2,1)} %gain_a.1, bf16[1280]{0:T(1024)(128)(2,1)} %gain_f.1, bf16[320,1280]{1,0:T(8,128)(2,1)} %bitcast.9, bf16[320,1280]{1,0:T(8,128)(2,1)} %bitcast.10, bf16[320,1280]{1,0:T(8,128)(2,1)} %bitcast.11, bf16[320,1280]{1,0:T(8,128)(2,1)} %wo.1, ...), custom_call_target="tpu_custom_call" | custom-call | tf_op jit(solution)/shard_map/pallas_call | solution.py:540
  63.8 1.6 %copy.15 = bf16[256,320]{0,1:T(8,128)(2,1)} copy(bf16[256,320]{0,1:T(8,128)(2,1)} %bitcast.13) | data formatting | bytes 327680
